TPU v7x, 32 devices: a whole 2x2x4 slice. The times are simulated.
32 devices in a mesh: grp: 2 (over x), date: 16 (over z, y, core).
Axes of the slice: x: 2, y: 2, z: 4, core: 2. Of those that a mesh axis runs over, the one named last changes fastest.
Arguments:
- amplitude: bfloat16 [32, 256, 1024], P('date', 'grp'), parts along dimension 1, may hold values from 0.01 to 600, as said below
- phase: bfloat16 [32, 256, 1024], P('date', 'grp'), parts along dimension 1, may hold values from -3.1416 to 3.1416
- offset_code: int32 [32, 5], P('date'), may hold values from 0 to 4, each once within a row
- look_half: int32 [256, 1024], P('grp'), parts along dimension 0, may hold values from 1 to 3
Outputs:
- filtered: bfloat16 [32, 5, 2, 256, 1024], P('date', None, None, 'grp'), parts along dimension 3
- coherence: bfloat16 [32, 5, 256, 1024], P('date', None, 'grp'), parts along dimension 2
There are 2 independent parts, one for each index of `grp`. A program takes and returns all parts, laid end to end along the dimension named above; an argument that names none is the same for every part. Nothing has to cross between parts.
Inputs may be any that keep to these rules, and one draw needn't show every extreme that they name: `offset_code`: each row holds every value 0 to 4 exactly once. `amplitude`: positive amplitudes.
All inputs are finite; a program needn't handle non-finite values.
Results may differ from a plain program's by a relative error of at most 0.0004.
Values may be sent and summed in bfloat16 or wider, within the bound.
No kernel may reach another device: no remote copies, remote signals or barrier semaphores. Data moves between devices by JAX's collectives and lax.ppermute only.
A program may use at most 128 MiB of HBM per device.

v0:
```python
import functools

import jax
import jax.numpy as jnp
import numpy as np
from jax import lax
from jax.experimental import pallas as pl
from jax.experimental.pallas import tpu as pltpu
from jax.sharding import PartitionSpec as P

REACH = 5
DISP_GAIN = 4.0
LANES = 128
CHUNK = 16

SIN_TERMS = (1.0, -1.0 / 6, 1.0 / 120, -1.0 / 5040, 1.0 / 362880, -1.0 / 39916800, 1.0 / 6227020800)
COS_TERMS = (1.0, -1.0 / 2, 1.0 / 24, -1.0 / 720, 1.0 / 40320, -1.0 / 3628800, 1.0 / 479001600)


def series(square, terms):
    total = jnp.full_like(square, terms[-1])
    for term in terms[-2::-1]:
        total = total * square + term
    return total


def slc_of(amplitude, phase):
    amplitude = amplitude.astype(jnp.float32)
    half = phase.astype(jnp.float32) * 0.5
    square = half * half
    sine = half * series(square, SIN_TERMS)
    cosine = series(square, COS_TERMS)
    scaled = (amplitude + amplitude) * sine
    return amplitude - scaled * sine, scaled * cosine


def trig_kernel(amp_ref, phase_ref, slc_ref):
    rows = amp_ref.shape[1]

    def step(index, carry):
        here = pl.ds(pl.multiple_of(index * CHUNK, CHUNK), CHUNK)
        real, imag = slc_of(amp_ref[0, here], phase_ref[0, here])
        slc_ref[0, 0, here] = real
        slc_ref[0, 1, here] = imag
        return carry

    lax.fori_loop(0, rows // CHUNK, step, 0)


def slc_tiles(amplitude, phase):
    dates, rows, cols = amplitude.shape
    block = pl.BlockSpec((1, rows, cols), lambda d: (d, 0, 0))
    return pl.pallas_call(
        trig_kernel,
        grid=(dates,),
        in_specs=[block, block],
        out_specs=pl.BlockSpec((1, 2, rows, cols), lambda d: (d, 0, 0, 0)),
        out_shape=jax.ShapeDtypeStruct((dates, 2, rows, cols), jnp.float32),
        cost_estimate=pl.CostEstimate(flops=dates * rows * cols * 40, bytes_accessed=dates * rows * cols * 12, transcendentals=0),
    )(amplitude, phase)


def beside(tiles, step):
    lane = lax.broadcasted_iota(jnp.int32, tiles[0].shape, 1)
    turned = [pltpu.roll(tile, (-step) % LANES, 1) for tile in tiles]
    count = len(tiles)
    out = []
    for c in range(count):
        if step > 0:
            other = turned[c + 1] if c + 1 < count else jnp.zeros_like(tiles[0])
            out.append(jnp.where(lane >= LANES - step, other, turned[c]))
        else:
            other = turned[c - 1] if c > 0 else jnp.zeros_like(tiles[0])
            out.append(jnp.where(lane < -step, other, turned[c]))
    return out


def put_column_sums(tiles, sums_ref, row, rows):
    total = tiles
    for j in (1, 2, 3):
        after = beside(tiles, j)
        before = beside(tiles, -j)
        total = [t + a + b for t, a, b in zip(total, after, before)]
        for c, value in enumerate(total):
            high = value.astype(jnp.bfloat16)
            low = (value - high.astype(jnp.float32)).astype(jnp.bfloat16)
            sums_ref[j - 1, pl.ds(row, CHUNK), c * LANES : (c + 1) * LANES] = high
            sums_ref[j - 1, pl.ds(rows + row, CHUNK), c * LANES : (c + 1) * LANES] = low


def looked(sums_ref, band_ref, half, columns):
    box = [
        jnp.dot(band_ref[h], sums_ref[h, :, columns], preferred_element_type=jnp.float32)
        for h in range(3)
    ]
    return jnp.where(half == 1, box[0], jnp.where(half == 2, box[1], box[2]))


def main_kernel(
    dates_dev, slot_ref, valid_ref, own_ref, far_ref, weight_ref, half_ref, band_ref,
    filtered_ref, gamma_ref, inverse_ref, sums_ref, unit_ref,
):
    rows, cols = weight_ref.shape
    tiles = cols // LANES
    wide = 2 * LANES
    ext = dates_dev + REACH
    step = pl.program_id(0)
    date = step // REACH
    offset = step % REACH + 1

    def tile_of(c):
        return slice(c * LANES, (c + 1) * LANES)

    @pl.when(step == 0)
    def _():
        unit_ref[:, :, 0:8, :] = jnp.zeros((2, tiles, 8, LANES), jnp.float32)
        unit_ref[:, :, rows + 8 : rows + 16, :] = jnp.zeros((2, tiles, 8, LANES), jnp.float32)

        def power_date(d, slc_ref, base):
            for row in range(0, rows, CHUNK):
                here = slice(row, row + CHUNK)
                power = []
                for c in range(tiles):
                    real = slc_ref[d, 0, here, tile_of(c)]
                    imag = slc_ref[d, 1, here, tile_of(c)]
                    power.append(weight_ref[here, tile_of(c)] * (real * real + imag * imag))
                put_column_sums(power, sums_ref.at[0], row, rows)
            valid = valid_ref[base + d] != 0
            for n in range(0, cols, wide):
                columns = slice(n, n + wide)
                power = looked(sums_ref.at[0], band_ref, half_ref[:, columns], columns)
                inverse_ref[base + d, :, columns] = jnp.where(valid, lax.rsqrt(power), 0.0)

        def own_power(d, carry):
            power_date(d, own_ref, 0)
            return carry

        def far_power(d, carry):
            power_date(d, far_ref, dates_dev)
            return carry

        lax.fori_loop(0, dates_dev, own_power, 0)
        lax.fori_loop(0, REACH, far_power, 0)

    far = date + offset

    def pair(other_ref, other):
        for row in range(0, rows, CHUNK):
            here = slice(row, row + CHUNK)
            reals, imags = [], []
            for c in range(tiles):
                weight = weight_ref[here, tile_of(c)]
                real = weight * own_ref[date, 0, here, tile_of(c)]
                imag = weight * own_ref[date, 1, here, tile_of(c)]
                far_real = other_ref[other, 0, here, tile_of(c)]
                far_imag = other_ref[other, 1, here, tile_of(c)]
                reals.append(real * far_real + imag * far_imag)
                imags.append(imag * far_real - real * far_imag)
            put_column_sums(reals, sums_ref.at[0], row, rows)
            put_column_sums(imags, sums_ref.at[1], row, rows)

    @pl.when(far < dates_dev)
    def _():
        pair(own_ref, far)

    @pl.when(far >= dates_dev)
    def _():
        pair(far_ref, far - dates_dev)

    for n in range(0, cols, wide):
        columns = slice(n, n + wide)
        half = half_ref[:, columns]
        scale = inverse_ref[date, :, columns] * inverse_ref[far, :, columns]
        for part in range(2):
            unit = looked(sums_ref.at[part], band_ref, half, columns) * scale
            for k in range(wide // LANES):
                unit_ref[part, n // LANES + k, 8 : rows + 8, :] = unit[:, tile_of(k)]

    for row in range(0, rows, CHUNK):
        units, means = [], []
        for part in range(2):
            centre = [unit_ref[part, c, row + 8 : row + 8 + CHUNK, :] for c in range(tiles)]
            column = [
                centre[c]
                + unit_ref[part, c, row + 7 : row + 7 + CHUNK, :]
                + unit_ref[part, c, row + 9 : row + 9 + CHUNK, :]
                for c in range(tiles)
            ]
            after, before = beside(column, 1), beside(column, -1)
            units.append(centre)
            means.append([(m + a + b) * (1.0 / 9.0) for m, a, b in zip(column, after, before)])
        for c in range(tiles):
            real, imag = units[0][c], units[1][c]
            gamma = jnp.sqrt(real * real + imag * imag)
            for part in range(2):
                mean = means[part][c]
                value = mean + gamma * (units[part][c] - mean)
                filtered_ref[0, 0, part, row : row + CHUNK, tile_of(c)] = value.astype(jnp.bfloat16)
            gamma_ref[0, 0, row : row + CHUNK, tile_of(c)] = gamma.astype(jnp.bfloat16)


def band_of(rows):
    gap = np.abs(np.arange(rows)[:, None] - np.arange(rows)[None, :])
    band = np.stack([(gap <= h).astype(np.float32) for h in (1, 2, 3)])
    return jnp.asarray(np.concatenate([band, band], axis=2), jnp.bfloat16)


def interferograms(own, far, weight, look_half, slot, valid):
    dates_dev, _, rows, cols = own.shape
    ext = dates_dev + REACH
    whole = pl.BlockSpec(memory_space=pltpu.VMEM)
    spec = pltpu.PrefetchScalarGridSpec(
        num_scalar_prefetch=2,
        grid=(dates_dev * REACH,),
        in_specs=[whole] * 5,
        out_specs=[
            pl.BlockSpec((1, 1, 2, rows, cols), lambda s, slot, valid: (s // REACH, slot[s], 0, 0, 0)),
            pl.BlockSpec((1, 1, rows, cols), lambda s, slot, valid: (s // REACH, slot[s], 0, 0)),
        ],
        scratch_shapes=[
            pltpu.VMEM((ext, rows, cols), jnp.float32),
            pltpu.VMEM((2, 3, 2 * rows, cols), jnp.bfloat16),
            pltpu.VMEM((2, cols // LANES, rows + 16, LANES), jnp.float32),
        ],
    )
    return pl.pallas_call(
        functools.partial(main_kernel, dates_dev),
        grid_spec=spec,
        out_shape=[
            jax.ShapeDtypeStruct((dates_dev, REACH, 2, rows, cols), jnp.bfloat16),
            jax.ShapeDtypeStruct((dates_dev, REACH, rows, cols), jnp.bfloat16),
        ],
        compiler_params=pltpu.CompilerParams(vmem_limit_bytes=48 * 2**20),
        cost_estimate=pl.CostEstimate(flops=10**10, bytes_accessed=2 * 10**7, transcendentals=10**6),
    )(slot, valid, own, far, weight, look_half, band_of(rows))


def from_behind(value, axis, steps):
    count = lax.axis_size(axis)
    return lax.ppermute(value, axis, [(source, source + steps) for source in range(max(0, -steps), min(count, count - steps))])


def weight_of(amplitude, total_dates):
    mine = lax.all_to_all(amplitude, "date", 1, 0, tiled=True).astype(jnp.float32)
    first = jnp.sum(mine, axis=0)
    second = jnp.sum(mine * mine, axis=0)
    weight = 1.0 / (1.0 + DISP_GAIN * (total_dates * second / (first * first) - 1.0))
    return lax.all_gather(weight, "date", axis=0, tiled=True)


def local(amplitude, phase, offset_code, look_half):
    dates_dev = amplitude.shape[0]
    total_dates = dates_dev * lax.axis_size("date")
    first_date = lax.axis_index("date") * dates_dev
    pieces = []
    for hop in range(1, (REACH + dates_dev - 1) // dates_dev + 1):
        take = min(dates_dev, REACH - (hop - 1) * dates_dev)
        pieces.append((from_behind(amplitude[:take], "date", -hop), from_behind(phase[:take], "date", -hop)))
    weight = weight_of(amplitude, total_dates)
    own = slc_tiles(amplitude, phase)
    far = slc_tiles(*(jnp.concatenate([piece[k] for piece in pieces]) for k in range(2)))
    valid = (first_date + jnp.arange(dates_dev + REACH) < total_dates).astype(jnp.int32)
    same = offset_code[:, None, :] == jnp.arange(REACH, dtype=jnp.int32)[None, :, None]
    slot = jnp.sum(jnp.where(same, jnp.arange(REACH, dtype=jnp.int32), 0), axis=2, dtype=jnp.int32).reshape(-1)
    filtered, coherence = interferograms(own, far, weight, look_half, slot, valid)
    return filtered, coherence


def solution(mesh):
    return jax.shard_map(
        local,
        mesh=mesh,
        in_specs=(P("date", "grp", None), P("date", "grp", None), P("date", None), P("grp", None)),
        out_specs=(P("date", None, None, "grp", None), P("date", None, "grp", None)),
        check_vma=False,
    )
```

profile of v0, /device:TPU:1, one launch (start us, length us, event | category | flops | bytes accessed | tf_op | source)
XLA Modules:
  0.0 139.9 jit_solution(15919713076268701743)
XLA Ops:
  0.6 0.0 copy-start.3
  0.6 0.0 copy-start.4
  0.7 0.0 copy-start.5
  0.7 2.5 %copy.9 = bf16[2,128,1024]{2,0,1:T(2,128)(2,1)} copy(bf16[2,128,1024]{2,1,0:T(8,128)(2,1)} %amp_ref.1) | data formatting | bytes 1048576 | tf_op args[0]
  3.1 7.3 %all-to-all-start = ((bf16[2,128,1024]{2,0,1:T(2,128)(2,1)}), bf16[2,128,1024]{2,0,1:T(2,128)(2,1)S(1)}, u32[]{:S(2)}, u32[]{:S(2)}) async-start(bf16[2,128,1024]{2,0,1:T(2,128)(2,1)} %copy.9), calls=%async_computation | async-start | bytes 1048576 | tf_op jit(solution)/shard_map/all_to_all | solution.py:244
  10.5 0.0 copy-done.4
  10.5 2.0 %collective-permute-start.3 = (bf16[2,128,1024]{2,1,0:T(8,128)(2,1)S(1)}, bf16[2,128,1024]{2,1,0:T(8,128)(2,1)S(1)}, u32[]{:S(2)}, u32[]{:S(2)}) collective-permute-start(bf16[2,128,1024]{2,1,0:T(8,128)(2,1)S(1)} %copy-done.4), channel_id=1, source_target_pairs={{1,0},{2,1},{3,2},{4,3},{5,4},{6,5},{7,6},{8,7},{9,8},{10,9},{11,1... | collective-permute-start | bytes 1572872 | tf_op jit(solution)/shard_map/ppermute | solution.py:240
  12.5 1.3 collective-permute-start.4
  13.8 1.3 collective-permute-start.5
  15.1 0.0 copy-done.3
  15.1 1.3 collective-permute-start.1
  16.4 1.9 %collective-permute-start = (bf16[2,128,1024]{2,1,0:T(8,128)(2,1)S(1)}, bf16[2,128,1024]{2,1,0:T(8,128)(2,1)S(1)}, u32[]{:S(2)}, u32[]{:S(2)}) collective-permute-start(bf16[2,128,1024]{2,1,0:T(8,128)(2,1)S(1)} %copy-done.3), channel_id=1, source_target_pairs={{1,0},{2,1},{3,2},{4,3},{5,4},{6,5},{7,6},{8,7},{9,8},{10,9},{11,1... | collective-permute-start | bytes 1572872 | tf_op jit(solution)/shard_map/ppermute | solution.py:240
  18.4 0.7 slice.6
  19.1 30.8 %collective-permute-done.5 = bf16[1,128,1024]{2,1,0:T(8,128)(2,1)} collective-permute-done((bf16[1,128,1024]{2,1,0:T(8,128)(2,1)S(1)}, bf16[1,128,1024]{2,1,0:T(8,128)(2,1)}, u32[]{:S(2)}, u32[]{:S(2)}) %collective-permute-start.5) | collective-permute-done | bytes 262176 | tf_op jit(solution)/shard_map/ppermute | solution.py:240
  49.9 1.3 collective-permute-start.2
  51.2 0.0 copy-done.5
  51.2 0.2 fusion.3
  51.4 0.1 copy.8
  51.5 0.1 reshape.10.slot_ref
  51.6 3.3 %shard_map.68.own_ref = f32[2,2,128,1024]{3,2,1,0:T(8,128)} custom-call(bf16[2,128,1024]{2,1,0:T(8,128)(2,1)} %amp_ref.1, bf16[2,128,1024]{2,1,0:T(8,128)(2,1)} %phase_ref.1), custom_call_target="tpu_custom_call" | custom-call | flops 10485760 | bytes 3145728 | tf_op jit(solution)/shard_map/pallas_call | solution.py:53
  54.9 0.0 collective-permute-done.3
  54.9 0.0 collective-permute-done.4
  55.0 2.4 %pad_maximum_fusion.1.phase_ref = bf16[5,128,1024]{2,1,0:T(8,128)(2,1)} fusion(bf16[1,128,1024]{2,1,0:T(8,128)(2,1)} %collective-permute-done.5, bf16[2,128,1024]{2,1,0:T(8,128)(2,1)} %collective-permute-done.4, bf16[2,128,1024]{2,1,0:T(8,128)(2,1)S(1)} %collective-permute-done.3), kind=kLoop, calls=%fused_computation.1 | loop fusion | flops 1310720 | bytes 2621440 | tf_op jit(solution)/shard_map/concatenate | solution.py:261
  57.3 9.1 %collective-permute-done.2 = bf16[1,128,1024]{2,1,0:T(8,128)(2,1)} collective-permute-done((bf16[1,128,1024]{2,1,0:T(8,128)(2,1)}, bf16[1,128,1024]{2,1,0:T(8,128)(2,1)}, u32[]{:S(2)}, u32[]{:S(2)}) %collective-permute-start.2) | collective-permute-done | bytes 262176 | tf_op jit(solution)/shard_map/ppermute | solution.py:240
  66.5 0.0 collective-permute-done.1
  66.5 0.0 collective-permute-done
  66.5 2.2 %pad_maximum_fusion.amp_ref = bf16[5,128,1024]{2,1,0:T(8,128)(2,1)} fusion(bf16[1,128,1024]{2,1,0:T(8,128)(2,1)} %collective-permute-done.2, bf16[2,128,1024]{2,1,0:T(8,128)(2,1)S(1)} %collective-permute-done.1, bf16[2,128,1024]{2,1,0:T(8,128)(2,1)S(1)} %collective-permute-done), kind=kLoop, calls=%fused_computation | loop fusion | flops 1310720 | bytes 2621440 | tf_op jit(solution)/shard_map/concatenate | solution.py:261
  68.7 7.0 %shard_map.69.far_ref = f32[5,2,128,1024]{3,2,1,0:T(8,128)} custom-call(bf16[5,128,1024]{2,1,0:T(8,128)(2,1)} %pad_maximum_fusion.amp_ref, bf16[5,128,1024]{2,1,0:T(8,128)(2,1)} %pad_maximum_fusion.1.phase_ref), custom_call_target="tpu_custom_call" | custom-call | flops 26214400 | bytes 7864320 | tf_op jit(solution)/shard_map/pallas_call | solution.py:53
  75.6 0.0 all-to-all-done
  75.6 0.9 fusion.2
  76.6 19.9 %all_gather.3.weight_ref = f32[128,1024]{1,0:T(8,128)S(1)} all-gather(f32[8,1024]{1,0:T(8,128)S(1)} %add_divide_fusion), channel_id=1, replica_groups=mesh['grp'=2,'date'=16] {'date'}, dimensions={0}, use_global_device_ids=true | all-gather | bytes 557056 | tf_op jit(solution)/shard_map/all_gather | solution.py:248
  96.5 43.4 %shard_map.70 = (bf16[2,5,2,128,1024]{4,3,2,1,0:T(8,128)(2,1)}, bf16[2,5,128,1024]{3,2,1,0:T(8,128)(2,1)}) custom-call(s32[10]{0:T(128)S(1)} %reshape.10.slot_ref, s32[7]{0:T(128)S(1)} %compare_convert_fusion.valid_ref, f32[2,2,128,1024]{3,2,1,0:T(8,128)S(1)} %copy-done, f32[5,2,128,1024]{3,2,1,0:T(8,128)} %shard_map.69.far_ref, ...), custom_call_target="tpu_custom_call" | custom-call | flops 10000000000 | bytes 20000000 | tf_op jit(solution)/shard_map/pallas_call | solution.py:226
  (9 shorter events, 0.1 us)
Async XLA Ops:
  0.6 14.5 %copy-start.3 = (bf16[2,128,1024]{2,1,0:T(8,128)(2,1)S(1)}, bf16[2,128,1024]{2,1,0:T(8,128)(2,1)}, u32[]{:S(2)}) copy-start(bf16[2,128,1024]{2,1,0:T(8,128)(2,1)} %amp_ref.1) | copy-start | bytes 1572868
  0.6 9.8 %copy-start.4 = (bf16[2,128,1024]{2,1,0:T(8,128)(2,1)S(1)}, bf16[2,128,1024]{2,1,0:T(8,128)(2,1)}, u32[]{:S(2)}) copy-start(bf16[2,128,1024]{2,1,0:T(8,128)(2,1)} %phase_ref.1) | copy-start | bytes 1572868
  0.7 50.6 %copy-start.5 = (s32[2,5]{1,0:T(2,128)S(1)}, s32[2,5]{1,0:T(2,128)}, u32[]{:S(2)}) copy-start(s32[2,5]{1,0:T(2,128)} %param.7) | copy-start | bytes 124
  3.1 72.5 %all-to-all-start = ((bf16[2,128,1024]{2,0,1:T(2,128)(2,1)}), bf16[2,128,1024]{2,0,1:T(2,128)(2,1)S(1)}, u32[]{:S(2)}, u32[]{:S(2)}) async-start(bf16[2,128,1024]{2,0,1:T(2,128)(2,1)} %copy.9), calls=%async_computation | async-start | bytes 1048576 | tf_op jit(solution)/shard_map/all_to_all | solution.py:244
  10.5 44.5 %collective-permute-start.3 = (bf16[2,128,1024]{2,1,0:T(8,128)(2,1)S(1)}, bf16[2,128,1024]{2,1,0:T(8,128)(2,1)S(1)}, u32[]{:S(2)}, u32[]{:S(2)}) collective-permute-start(bf16[2,128,1024]{2,1,0:T(8,128)(2,1)S(1)} %copy-done.4), channel_id=1, source_target_pairs={{1,0},{2,1},{3,2},{4,3},{5,4},{6,5},{7,6},{8,7},{9,8},{10,9},{11,1... | collective-permute-start | bytes 1572872 | tf_op jit(solution)/shard_map/ppermute | solution.py:240
  12.5 42.4 %collective-permute-start.4 = (bf16[2,128,1024]{2,1,0:T(8,128)(2,1)S(1)}, bf16[2,128,1024]{2,1,0:T(8,128)(2,1)}, u32[]{:S(2)}, u32[]{:S(2)}) collective-permute-start(bf16[2,128,1024]{2,1,0:T(8,128)(2,1)S(1)} %copy-done.4), channel_id=1, source_target_pairs={{2,0},{3,1},{4,2},{5,3},{6,4},{7,5},{8,6},{9,7},{10,8},{11,9},{12,... | collective-permute-start | bytes 1572872 | tf_op jit(solution)/shard_map/ppermute | solution.py:240
  13.8 36.1 %collective-permute-start.5 = (bf16[1,128,1024]{2,1,0:T(8,128)(2,1)S(1)}, bf16[1,128,1024]{2,1,0:T(8,128)(2,1)}, u32[]{:S(2)}, u32[]{:S(2)}) collective-permute-start(bf16[1,128,1024]{2,1,0:T(8,128)(2,1)S(1)} %slice.7), channel_id=1, source_target_pairs={{3,0},{4,1},{5,2},{6,3},{7,4},{8,5},{9,6},{10,7},{11,8},{12,9},{13... | collective-permute-start | bytes 786440 | tf_op jit(solution)/shard_map/ppermute | solution.py:240
  15.1 51.4 %collective-permute-start.1 = (bf16[2,128,1024]{2,1,0:T(8,128)(2,1)S(1)}, bf16[2,128,1024]{2,1,0:T(8,128)(2,1)S(1)}, u32[]{:S(2)}, u32[]{:S(2)}) collective-permute-start(bf16[2,128,1024]{2,1,0:T(8,128)(2,1)S(1)} %copy-done.3), channel_id=1, source_target_pairs={{2,0},{3,1},{4,2},{5,3},{6,4},{7,5},{8,6},{9,7},{10,8},{11,9},{12,... | collective-permute-start | bytes 1572872 | tf_op jit(solution)/shard_map/ppermute | solution.py:240
  16.4 50.1 %collective-permute-start = (bf16[2,128,1024]{2,1,0:T(8,128)(2,1)S(1)}, bf16[2,128,1024]{2,1,0:T(8,128)(2,1)S(1)}, u32[]{:S(2)}, u32[]{:S(2)}) collective-permute-start(bf16[2,128,1024]{2,1,0:T(8,128)(2,1)S(1)} %copy-done.3), channel_id=1, source_target_pairs={{1,0},{2,1},{3,2},{4,3},{5,4},{6,5},{7,6},{8,7},{9,8},{10,9},{11,1... | collective-permute-start | bytes 1572872 | tf_op jit(solution)/shard_map/ppermute | solution.py:240
  49.9 16.6 %collective-permute-start.2 = (bf16[1,128,1024]{2,1,0:T(8,128)(2,1)}, bf16[1,128,1024]{2,1,0:T(8,128)(2,1)}, u32[]{:S(2)}, u32[]{:S(2)}) collective-permute-start(bf16[1,128,1024]{2,1,0:T(8,128)(2,1)} %slice.6), channel_id=1, source_target_pairs={{3,0},{4,1},{5,2},{6,3},{7,4},{8,5},{9,6},{10,7},{11,8},{12,9},{13... | collective-permute-start | bytes 786440 | tf_op jit(solution)/shard_map/ppermute | solution.py:240
  68.7 27.8 %copy-start = (f32[2,2,128,1024]{3,2,1,0:T(8,128)S(1)}, f32[2,2,128,1024]{3,2,1,0:T(8,128)}, u32[]{:S(2)}) copy-start(f32[2,2,128,1024]{3,2,1,0:T(8,128)} %shard_map.68.own_ref) | copy-start | bytes 6291460
  68.7 27.8 %copy-start.1 = (s32[128,1024]{1,0:T(8,128)S(1)}, s32[128,1024]{1,0:T(8,128)}, u32[]{:S(2)}) copy-start(s32[128,1024]{1,0:T(8,128)} %half_ref.1) | copy-start | bytes 1572868
  68.7 27.8 %copy-start.2 = (bf16[3,128,256]{2,1,0:T(8,128)(2,1)S(1)}, bf16[3,128,256]{2,1,0:T(8,128)(2,1)}, u32[]{:S(2)}) copy-start(bf16[3,128,256]{2,1,0:T(8,128)(2,1)} %constant.22.clone.band_ref) | copy-start | bytes 589828
where the time goes:
time: 141 us; the launch traced here: 140 us
  Pallas kernels  53.7 us (38%)
  waiting for transfers between devices  40 us (28%)
  blocking collectives  19.9 us (14%)
  starting transfers between devices  16.4 us (12%)
  other arithmetic  5.66 us (4%)
  local copies, waits for them, and re-layouts  3.41 us (2%)
    pallas_call x1, Pallas kernels, interferograms(): pl.pallas_call(functools.partial(main_kernel, dates_dev), grid_spec=spec,...  43.4 us
    ppermute x6, waiting for transfers between devices, from_behind(): lax.ppermute(value, axis, [(source, source + steps) for source in range(m...  40 us
    all_gather x1, blocking collectives, weight_of(): return lax.all_gather(weight, 'date', axis=0, tiled=True)  19.9 us
    pallas_call x2, Pallas kernels, slc_tiles(): pl.pallas_call(trig_kernel, grid=(dates,), in_specs=[block, block], out_s...  10.3 us
    ppermute x6, starting transfers between devices, from_behind(): lax.ppermute(value, axis, [(source, source + steps) for source in range(m...  9.09 us
    all_to_all x1, starting transfers between devices, weight_of(): lax.all_to_all(amplitude, 'date', 1, 0, tiled=True).astype(jnp.float32)  7.35 us
    concatenate x2, other arithmetic, local(): jnp.concatenate([piece[k] for piece in pieces])  4.55 us
  transfers between devices with their start and end apart: 7, of which 2 were waited for; matrix products, arithmetic and copies ran while one was open for 4% of the time, Pallas kernels for 7%

commit v1 on v0

v1 whole, which is shorter than its diff:
```python
import functools

import jax
import jax.numpy as jnp
import numpy as np
from jax import lax
from jax.experimental import pallas as pl
from jax.experimental.pallas import tpu as pltpu
from jax.sharding import PartitionSpec as P

REACH = 5
DISP_GAIN = 4.0
LANES = 128
CHUNK = 16
PAD = 8

SIN_TERMS = (1.0, -1.0 / 6, 1.0 / 120, -1.0 / 5040, 1.0 / 362880, -1.0 / 39916800, 1.0 / 6227020800)
COS_TERMS = (1.0, -1.0 / 2, 1.0 / 24, -1.0 / 720, 1.0 / 40320, -1.0 / 3628800, 1.0 / 479001600)


def series(square, terms):
    total = jnp.full_like(square, terms[-1])
    for term in terms[-2::-1]:
        total = total * square + term
    return total


def slc_of(amplitude, phase):
    amplitude = amplitude.astype(jnp.float32)
    half = phase.astype(jnp.float32) * 0.5
    square = half * half
    sine = half * series(square, SIN_TERMS)
    cosine = series(square, COS_TERMS)
    scaled = (amplitude + amplitude) * sine
    return amplitude - scaled * sine, scaled * cosine


def over_rows(rows, body):
    def step(index, carry):
        body(pl.ds(pl.multiple_of(index * CHUNK, CHUNK), CHUNK))
        return carry

    lax.fori_loop(0, rows // CHUNK, step, 0)


def cost(pixels, flops, nbytes):
    return pl.CostEstimate(flops=pixels * flops, bytes_accessed=pixels * nbytes, transcendentals=0)


VMEM = pl.BlockSpec(memory_space=pltpu.VMEM)
SMEM = pl.BlockSpec(memory_space=pltpu.SMEM)


def slc_dates(place_ref, sources, slc_ref):
    odd = place_ref[0] != 0

    def body(n, carry):
        columns = pl.ds(pl.multiple_of(n * LANES, LANES), LANES)
        for date, pair, index, other, other_index in sources:
            found = []
            for k in range(2):
                value = pair[k][index, :, columns].astype(jnp.float32)
                if other is not None:
                    value = jnp.where(odd, value, other[k][other_index, :, columns].astype(jnp.float32))
                found.append(value.T)
            slc_ref[date, 0, columns], slc_ref[date, 1, columns] = slc_of(*found)
        return carry

    lax.fori_loop(0, sources[0][1][0].shape[2] // LANES, body, 0)


def first_slc_kernel(place_ref, own_amp, own_phase, next_amp, next_phase, slc_ref):
    own, following = (own_amp, own_phase), (next_amp, next_phase)
    slc_dates(
        place_ref,
        [(0, own, 0, None, 0), (1, own, 1, None, 0), (4, following, 0, None, 0), (5, following, 1, None, 0)],
        slc_ref,
    )


def second_slc_kernel(place_ref, mate_amp, mate_phase, via_amp, via_phase, last_ref, begun_ref, slc_ref):
    mate, via, last = (mate_amp, mate_phase), (via_amp, via_phase), (last_ref.at[0:1], last_ref.at[1:2])
    slc_dates(place_ref, [(2, via, 0, mate, 0), (3, via, 1, mate, 1), (6, last, 0, via, 0)], slc_ref)


def slc_turned(kernel, place, *arrays, begun=None):
    dates, rows, cols = arrays[0].shape
    if begun is not None:
        arrays = arrays + (begun,)
    return pl.pallas_call(
        kernel,
        in_specs=[SMEM] + [VMEM] * len(arrays),
        out_specs=VMEM,
        out_shape=jax.ShapeDtypeStruct((dates + REACH, 2, cols, rows), jnp.float32),
        input_output_aliases={} if begun is None else {len(arrays): 0},
        compiler_params=pltpu.CompilerParams(vmem_limit_bytes=16 * 2**20),
        cost_estimate=cost(dates * rows * cols, 8000, 12),
    )(place, *arrays)


def gate_kernel(*refs):
    pass


def after(values, *others):
    ANY = pl.BlockSpec(memory_space=pl.ANY)
    return pl.pallas_call(
        gate_kernel,
        in_specs=[ANY] * (len(values) + len(others)),
        out_specs=[ANY] * len(values),
        out_shape=[jax.ShapeDtypeStruct(v.shape, v.dtype) for v in values],
        input_output_aliases={k: k for k in range(len(values))},
    )(*values, *others)


def moments_kernel(place_ref, own_ref, mate_ref, phase_ref, pieces_ref, early_ref):
    chips, _, deep, cols = pieces_ref.shape
    half = chips * deep
    start = place_ref[0] * half
    early_ref[0] = own_ref[0]
    early_ref[1] = phase_ref[0]

    for row in range(0, half, CHUNK):
        there = pl.ds(pl.multiple_of(start + row, CHUNK), CHUNK)
        values = [ref[d, there].astype(jnp.float32) for ref in (own_ref, mate_ref) for d in range(ref.shape[0])]
        squares = [v * v for v in values]
        for which, total in enumerate((sum(values[1:], values[0]), sum(squares[1:], squares[0]))):
            for low in range(0, CHUNK, min(deep, CHUNK)):
                chip, inside = (row + low) // deep, (row + low) % deep
                size = min(deep, CHUNK)
                pieces_ref[chip, which, inside : inside + size] = total[low : low + size]


def moment_pieces(place, own, mate, phase, chips):
    _, rows, cols = own.shape
    half = rows // 2
    return pl.pallas_call(
        moments_kernel,
        in_specs=[SMEM, VMEM, VMEM, VMEM],
        out_specs=[VMEM, VMEM],
        out_shape=[
            jax.ShapeDtypeStruct((chips, 2, half // chips, cols), jnp.float32),
            jax.ShapeDtypeStruct((2, rows, cols), jnp.bfloat16),
        ],
        cost_estimate=cost(half * cols, 12, 24),
    )(place, own, mate, phase)


def beside(tiles, step):
    lane = lax.broadcasted_iota(jnp.int32, tiles[0].shape, 1)
    turned = [pltpu.roll(tile, (-step) % LANES, 1) for tile in tiles]
    count = len(tiles)
    out = []
    for c in range(count):
        if step > 0:
            other = turned[c + 1] if c + 1 < count else jnp.zeros_like(tiles[0])
            out.append(jnp.where(lane >= LANES - step, other, turned[c]))
        else:
            other = turned[c - 1] if c > 0 else jnp.zeros_like(tiles[0])
            out.append(jnp.where(lane < -step, other, turned[c]))
    return out


def put_column_sums(field_ref, sums_ref):
    cols, rows = sums_ref.shape[1], sums_ref.shape[2] // 2
    for c in range(0, cols, CHUNK):
        total = field_ref[PAD + c : PAD + c + CHUNK]
        for j in (1, 2, 3):
            total = total + (field_ref[PAD + c + j : PAD + c + j + CHUNK] + field_ref[PAD + c - j : PAD + c - j + CHUNK])
            high = total.astype(jnp.bfloat16)
            sums_ref[j - 1, c : c + CHUNK, :rows] = high
            sums_ref[j - 1, c : c + CHUNK, rows:] = (total - high.astype(jnp.float32)).astype(jnp.bfloat16)


def looked(sums_ref, band_ref, half, columns):
    box = [
        lax.dot_general(band_ref[h], sums_ref[h, columns, :], (((1,), (1,)), ((), ())), preferred_element_type=jnp.float32)
        for h in range(3)
    ]
    return jnp.where(half == 1, box[0], jnp.where(half == 2, box[1], box[2]))


def main_kernel(
    dates_dev, slot_ref, valid_ref, place_ref, slc_ref, mine_ref, other_half_ref, half_ref, band_ref,
    filtered_ref, gamma_ref, flat_ref, weight_ref, inverse_ref, field_ref, sums_ref, unit_ref,
):
    cols, rows = weight_ref.shape
    tiles = cols // LANES
    wide = 2 * LANES
    step = pl.program_id(0)
    date = step // REACH
    far = date + step % REACH + 1

    def tile_of(c):
        return slice(c * LANES, (c + 1) * LANES)

    @pl.when(step == 0)
    def _():
        unit_ref[:, :, 0:PAD, :] = jnp.zeros((2, tiles, PAD, LANES), jnp.float32)
        unit_ref[:, :, rows + PAD : rows + 2 * PAD, :] = jnp.zeros((2, tiles, PAD, LANES), jnp.float32)
        field_ref[:, 0:PAD, :] = jnp.zeros((2, PAD, rows), jnp.float32)
        field_ref[:, cols + PAD : cols + 2 * PAD, :] = jnp.zeros((2, PAD, rows), jnp.float32)
        part = rows // 2
        start = pl.multiple_of(place_ref[0] * part, part)
        flat_ref[pl.ds(start, part), :] = mine_ref[...]
        flat_ref[pl.ds(pl.multiple_of(part - start, part), part), :] = other_half_ref[...]
        for c in range(tiles):
            weight_ref[tile_of(c)] = flat_ref[:, tile_of(c)].T

        def power_date(d, carry):
            for c in range(tiles):
                real, imag = slc_ref[d, 0, tile_of(c)], slc_ref[d, 1, tile_of(c)]
                field_ref[0, PAD + c * LANES : PAD + (c + 1) * LANES] = weight_ref[tile_of(c)] * (real * real + imag * imag)
            put_column_sums(field_ref.at[0], sums_ref.at[0])
            valid = valid_ref[d] != 0
            for n in range(0, cols, wide):
                columns = slice(n, n + wide)
                power = looked(sums_ref.at[0], band_ref, half_ref[:, columns], columns)
                inverse_ref[d, :, columns] = jnp.where(valid, lax.rsqrt(power), 0.0)
            return carry

        lax.fori_loop(0, dates_dev + REACH, power_date, 0)

    for c in range(0, cols, 4 * CHUNK):
        here = slice(c, c + 4 * CHUNK)
        weight = weight_ref[here]
        real, imag = weight * slc_ref[date, 0, here], weight * slc_ref[date, 1, here]
        far_real, far_imag = slc_ref[far, 0, here], slc_ref[far, 1, here]
        there = slice(PAD + c, PAD + c + 4 * CHUNK)
        field_ref[0, there] = real * far_real + imag * far_imag
        field_ref[1, there] = imag * far_real - real * far_imag
    for part in range(2):
        put_column_sums(field_ref.at[part], sums_ref.at[part])

    for n in range(0, cols, wide):
        columns = slice(n, n + wide)
        half = half_ref[:, columns]
        scale = inverse_ref[date, :, columns] * inverse_ref[far, :, columns]
        for part in range(2):
            unit = looked(sums_ref.at[part], band_ref, half, columns) * scale
            for k in range(wide // LANES):
                unit_ref[part, n // LANES + k, PAD : rows + PAD, :] = unit[:, tile_of(k)]

    for row in range(0, rows, CHUNK):
        units, means = [], []
        for part in range(2):
            centre = [unit_ref[part, c, row + PAD : row + PAD + CHUNK, :] for c in range(tiles)]
            column = [
                centre[c]
                + unit_ref[part, c, row + PAD - 1 : row + PAD - 1 + CHUNK, :]
                + unit_ref[part, c, row + PAD + 1 : row + PAD + 1 + CHUNK, :]
                for c in range(tiles)
            ]
            after, before = beside(column, 1), beside(column, -1)
            units.append(centre)
            means.append([(m + a + b) * (1.0 / 9.0) for m, a, b in zip(column, after, before)])
        for c in range(tiles):
            real, imag = units[0][c], units[1][c]
            gamma = jnp.sqrt(real * real + imag * imag)
            for part in range(2):
                mean = means[part][c]
                value = mean + gamma * (units[part][c] - mean)
                filtered_ref[0, 0, part, row : row + CHUNK, tile_of(c)] = value.astype(jnp.bfloat16)
            gamma_ref[0, 0, row : row + CHUNK, tile_of(c)] = gamma.astype(jnp.bfloat16)


def band_of(rows):
    gap = np.abs(np.arange(rows)[:, None] - np.arange(rows)[None, :])
    band = np.stack([(gap <= h).astype(np.float32) for h in (1, 2, 3)])
    return jnp.asarray(np.concatenate([band, band], axis=2), jnp.bfloat16)


def interferograms(place, slc, weights, look_half, slot, valid):
    ext, _, cols, rows = slc.shape
    dates_dev = ext - REACH
    whole = pl.BlockSpec(memory_space=pltpu.VMEM)
    spec = pltpu.PrefetchScalarGridSpec(
        num_scalar_prefetch=3,
        grid=(dates_dev * REACH,),
        in_specs=[whole] * 5,
        out_specs=[
            pl.BlockSpec((1, 1, 2, rows, cols), lambda s, slot, valid, place: (s // REACH, slot[s], 0, 0, 0)),
            pl.BlockSpec((1, 1, rows, cols), lambda s, slot, valid, place: (s // REACH, slot[s], 0, 0)),
        ],
        scratch_shapes=[
            pltpu.VMEM((rows, cols), jnp.float32),
            pltpu.VMEM((cols, rows), jnp.float32),
            pltpu.VMEM((ext, rows, cols), jnp.float32),
            pltpu.VMEM((2, cols + 2 * PAD, rows), jnp.float32),
            pltpu.VMEM((2, 3, cols, 2 * rows), jnp.bfloat16),
            pltpu.VMEM((2, cols // LANES, rows + 2 * PAD, LANES), jnp.float32),
        ],
    )
    return pl.pallas_call(
        functools.partial(main_kernel, dates_dev),
        grid_spec=spec,
        out_shape=[
            jax.ShapeDtypeStruct((dates_dev, REACH, 2, rows, cols), jnp.bfloat16),
            jax.ShapeDtypeStruct((dates_dev, REACH, rows, cols), jnp.bfloat16),
        ],
        compiler_params=pltpu.CompilerParams(vmem_limit_bytes=24 * 2**20),
        cost_estimate=pl.CostEstimate(flops=10**10, bytes_accessed=2 * 10**7, transcendentals=10**6),
    )(slot, valid, place, slc, *weights, look_half, band_of(rows))


def send(value, pairs):
    return lax.ppermute(value, "date", pairs)


def spread_weight(first, second, total_dates):
    return 1.0 / (1.0 + DISP_GAIN * (total_dates * second / (first * first) - 1.0))


def local(amplitude, phase, offset_code, look_half):
    dates_dev, rows, cols = amplitude.shape
    count = lax.axis_size("date")
    chips = count // 2
    total_dates = dates_dev * count
    index = lax.axis_index("date")
    place = jnp.stack([index % 2, index // 2]).astype(jnp.int32)
    mate_pairs = [(i, i ^ 1) for i in range(count)]
    to_even = [(i, i - 1) for i in range(1, count, 2)]
    next_pairs = [(i, i - 2) for i in range(2, count)]
    last_pairs = [(i, i - 3) for i in range(4, count, 2)]
    groups = [[core + 2 * chip for chip in range(chips)] for core in range(2)]

    amp_mate = send(amplitude, mate_pairs)
    pieces, early = moment_pieces(place, amplitude, amp_mate, phase, chips)
    moments = jnp.sum(lax.all_to_all(pieces, "date", 0, 0, axis_index_groups=groups), axis=0)
    following = [send(x, next_pairs) for x in (amplitude, phase)]
    last = send(early, last_pairs)
    phase_mate = send(phase, to_even)
    weight = spread_weight(moments[0], moments[1], total_dates)
    copies = jnp.broadcast_to(weight[None], (chips,) + weight.shape)
    mine = lax.all_to_all(copies, "date", 0, 0, axis_index_groups=groups).reshape(rows // 2, cols)
    following = after(following, copies)
    via = [send(x, mate_pairs) for x in following]
    weights = (mine, send(mine, mate_pairs))
    near = slc_turned(first_slc_kernel, place, amplitude, phase, *following)
    slc = slc_turned(second_slc_kernel, place, amp_mate, phase_mate, *via, last, begun=near)
    valid = (index * dates_dev + jnp.arange(dates_dev + REACH) < total_dates).astype(jnp.int32)
    same = offset_code[:, None, :] == jnp.arange(REACH, dtype=jnp.int32)[None, :, None]
    slot = jnp.sum(jnp.where(same, jnp.arange(REACH, dtype=jnp.int32), 0), axis=2, dtype=jnp.int32).reshape(-1)
    filtered, coherence = interferograms(place, slc, weights, look_half, slot, valid)
    return filtered, coherence


def solution(mesh):
    return jax.shard_map(
        local,
        mesh=mesh,
        in_specs=(P("date", "grp", None), P("date", "grp", None), P("date", None), P("grp", None)),
        out_specs=(P("date", None, None, "grp", None), P("date", None, "grp", None)),
        check_vma=False,
    )
```

time: 141 us -> 100 us (0.71)
  blocking collectives: 19.9 us -> 0 us
  Pallas kernels: 53.7 us -> 40 us
  waiting for transfers between devices: 40 us -> 28 us
  starting transfers between devices: 16.4 us -> 21.9 us
  other arithmetic: 5.66 us -> 1.57 us
  local copies, waits for them, and re-layouts: 3.41 us -> 7.38 us
    ppermute x6 -> x8, waiting for transfers between devices: 40 us -> 10.7 us  [send(): return lax.ppermute(value, 'date', pairs)]
    all_gather x1 -> x0, blocking collectives: 19.9 us -> none  [weight_of(): return lax.all_gather(weight, 'date', axis=0, tiled=True)]
    all_to_all x1 -> x2, waiting for transfers between devices: 0.01 us -> 17.3 us  [the longest x1 10.7 us: local(): lax.all_to_all(pieces, 'date', 0, 0, axis_index_groups=groups)]
    pallas_call x1, Pallas kernels: 43.4 us -> 30.9 us  [interferograms(): pl.pallas_call(functools.partial(main_kernel, dates_dev), grid_spec=spec,...]
    concatenate x2 -> x0, other arithmetic: 4.55 us -> none  [local(): jnp.concatenate([piece[k] for piece in pieces])]
    all_to_all x1 -> x2, starting transfers between devices: 7.35 us -> 11.8 us  [the longest x1 6.82 us: local(): lax.all_to_all(pieces, 'date', 0, 0, axis_index_groups=groups)]
    unnamed x13 -> x24, local copies, waits for them, and re-layouts: 2.49 us -> 6.46 us
    pallas_call x2 -> x4, Pallas kernels: 10.3 us -> 9.15 us  [the longest x2 6.74 us: slc_turned(): pl.pallas_call(kernel, in_specs=[SMEM] + [VMEM] * len(arrays), out_specs=...]
  transfers between devices with their start and end apart: 7 -> 10, of which waited for: 2 -> 4; matrix products, arithmetic and copies ran while one was open for 4% -> 2% of each run, Pallas kernels for 7% -> 7%
where the time goes in v1:
time: 100 us; the launch traced here: 99.7 us
  Pallas kernels  40 us (40%)
  waiting for transfers between devices  28 us (28%)
  starting transfers between devices  21.9 us (22%)
  local copies, waits for them, and re-layouts  7.38 us (7%)
  other arithmetic  1.57 us (2%)
    pallas_call x1, Pallas kernels, interferograms(): pl.pallas_call(functools.partial(main_kernel, dates_dev), grid_spec=spec,...  30.9 us
    all_to_all x1, waiting for transfers between devices, local(): lax.all_to_all(pieces, 'date', 0, 0, axis_index_groups=groups)  10.7 us
    ppermute x8, waiting for transfers between devices, send(): return lax.ppermute(value, 'date', pairs)  10.7 us
    ppermute x8, starting transfers between devices, send(): return lax.ppermute(value, 'date', pairs)  10.1 us
    all_to_all x1, starting transfers between devices, local(): lax.all_to_all(pieces, 'date', 0, 0, axis_index_groups=groups)  6.82 us
    pallas_call x2, Pallas kernels, slc_turned(): pl.pallas_call(kernel, in_specs=[SMEM] + [VMEM] * len(arrays), out_specs=...  6.74 us
    all_to_all x1, waiting for transfers between devices, local(): lax.all_to_all(copies, 'date', 0, 0, axis_index_groups=groups)  6.56 us
    unnamed x24, local copies, waits for them, and re-layouts  6.46 us
  transfers between devices with their start and end apart: 10, of which 4 were waited for; matrix products, arithmetic and copies ran while one was open for 2% of the time, Pallas kernels for 7%

profile of v1, /device:TPU:1, one launch (start us, length us, event | category | flops | bytes accessed | tf_op | source)
XLA Modules:
  0.0 99.7 jit_solution(17632717003508996108)
XLA Ops:
  0.6 0.1 collective-permute-start
  0.8 0.7 pad_add_fusion.place_ref
  1.4 1.4 %collective-permute-done.mate_ref.mate_amp = bf16[2,128,1024]{2,1,0:T(8,128)(2,1)S(1)} collective-permute-done((bf16[2,128,1024]{2,1,0:T(8,128)(2,1)}, bf16[2,128,1024]{2,1,0:T(8,128)(2,1)S(1)}, u32[]{:S(2)}, u32[]{:S(2)}) %collective-permute-start) | collective-permute-done | bytes 524320 | tf_op jit(solution)/shard_map/ppermute | solution.py:307
  2.8 0.8 copy-done.2
  3.6 2.4 %shard_map.68 = (f32[8,2,8,1024]{3,2,1,0:T(8,128)}, bf16[2,128,1024]{2,1,0:T(8,128)(2,1)}) custom-call(s32[2]{0:T(128)} %pad_add_fusion.place_ref, bf16[2,128,1024]{2,1,0:T(8,128)(2,1)} %own_amp.1, bf16[2,128,1024]{2,1,0:T(8,128)(2,1)} %copy-done.2, bf16[2,128,1024]{2,1,0:T(8,128)(2,1)} %own_phase.1), custom_call_target="tpu_custom_call" | custom-call | flops 786432 | bytes 1572864 | tf_op jit(solution)/shard_map/pallas_call | solution.py:137
  6.0 6.8 %all-to-all-start = ((f32[8,2,8,1024]{3,2,1,0:T(8,128)}), f32[8,2,8,1024]{3,2,1,0:T(8,128)S(1)}, u32[]{:S(2)}, u32[]{:S(2)}) async-start(f32[8,2,8,1024]{3,2,1,0:T(8,128)} %get-tuple-element.6), calls=%async_computation | async-start | bytes 1048576 | tf_op jit(solution)/shard_map/all_to_all | solution.py:329
  12.8 1.3 %collective-permute-start.2 = (bf16[2,128,1024]{2,1,0:T(8,128)(2,1)}, bf16[2,128,1024]{2,1,0:T(8,128)(2,1)S(1)}, u32[]{:S(2)}, u32[]{:S(2)}) collective-permute-start(bf16[2,128,1024]{2,1,0:T(8,128)(2,1)} %own_amp.1), channel_id=1, source_target_pairs={{2,0},{3,1},{4,2},{5,3},{6,4},{7,5},{8,6},{9,7},{10,8},{11,9},{12,... | collective-permute-start | bytes 1572872 | tf_op jit(solution)/shard_map/ppermute | solution.py:307
  14.1 1.3 %collective-permute-start.3 = (bf16[2,128,1024]{2,1,0:T(8,128)(2,1)}, bf16[2,128,1024]{2,1,0:T(8,128)(2,1)S(1)}, u32[]{:S(2)}, u32[]{:S(2)}) collective-permute-start(bf16[2,128,1024]{2,1,0:T(8,128)(2,1)} %own_phase.1), channel_id=1, source_target_pairs={{2,0},{3,1},{4,2},{5,3},{6,4},{7,5},{8,6},{9,7},{10,8},{11,9},{12,... | collective-permute-start | bytes 1572872 | tf_op jit(solution)/shard_map/ppermute | solution.py:307
  15.4 10.7 %all-to-all-done = f32[8,2,8,1024]{3,2,1,0:T(8,128)S(1)} async-done(((f32[8,2,8,1024]{3,2,1,0:T(8,128)}), f32[8,2,8,1024]{3,2,1,0:T(8,128)S(1)}, u32[]{:S(2)}, u32[]{:S(2)}) %all-to-all-start) | async-done | bytes 524320 | tf_op jit(solution)/shard_map/all_to_all | solution.py:329
  26.2 0.7 broadcast_in_dim.21.refs_2_
  27.0 5.0 %all-to-all-start.1 = ((f32[8,8,1024]{2,1,0:T(8,128)}), f32[8,8,1024]{2,1,0:T(8,128)S(1)}, u32[]{:S(2)}, u32[]{:S(2)}) async-start(f32[8,8,1024]{2,1,0:T(8,128)} %broadcast_in_dim.21.refs_2_), calls=%async_computation.1 | async-start | bytes 524288 | tf_op jit(solution)/shard_map/all_to_all | solution.py:335
  32.0 3.6 %collective-permute-start.1 = (bf16[2,128,1024]{2,1,0:T(8,128)(2,1)}, bf16[2,128,1024]{2,1,0:T(8,128)(2,1)S(1)}, u32[]{:S(2)}, u32[]{:S(2)}) collective-permute-start(bf16[2,128,1024]{2,1,0:T(8,128)(2,1)} %own_phase.1), channel_id=1, source_target_pairs={{1,0},{3,2},{5,4},{7,6},{9,8},{11,10},{13,12},{15,14},{17,16},{19,... | collective-permute-start | bytes 1572872 | tf_op jit(solution)/shard_map/ppermute | solution.py:307
  35.6 1.3 %collective-permute-start.6 = (bf16[2,128,1024]{2,1,0:T(8,128)(2,1)}, bf16[2,128,1024]{2,1,0:T(8,128)(2,1)S(1)}, u32[]{:S(2)}, u32[]{:S(2)}) collective-permute-start(bf16[2,128,1024]{2,1,0:T(8,128)(2,1)} %get-tuple-element.9), channel_id=1, source_target_pairs={{4,1},{6,3},{8,5},{10,7},{12,9},{14,11},{20,17},{22,19},{24,21},{2... | collective-permute-start | bytes 1572872 | tf_op jit(solution)/shard_map/ppermute | solution.py:307
  36.9 0.0 copy-start.4
  36.9 9.3 %collective-permute-done.3.refs_1_ = bf16[2,128,1024]{2,1,0:T(8,128)(2,1)S(1)} collective-permute-done((bf16[2,128,1024]{2,1,0:T(8,128)(2,1)}, bf16[2,128,1024]{2,1,0:T(8,128)(2,1)S(1)}, u32[]{:S(2)}, u32[]{:S(2)}) %collective-permute-start.3) | collective-permute-done | bytes 524320 | tf_op jit(solution)/shard_map/ppermute | solution.py:307
  46.2 0.8 copy-done.6
  47.0 0.7 collective-permute-start.4
  47.7 0.8 fusion.6
  48.5 0.1 copy.10
  48.6 0.1 reshape.11.slot_ref
  48.7 6.6 %all-to-all-done.1 = f32[8,8,1024]{2,1,0:T(8,128)S(1)} async-done(((f32[8,8,1024]{2,1,0:T(8,128)}), f32[8,8,1024]{2,1,0:T(8,128)S(1)}, u32[]{:S(2)}, u32[]{:S(2)}) %all-to-all-start.1) | async-done | bytes 262176 | tf_op jit(solution)/shard_map/all_to_all | solution.py:335
  55.3 1.8 %collective-permute-start.7 = (f32[64,1024]{1,0:T(8,128)S(1)}, f32[64,1024]{1,0:T(8,128)S(1)}, u32[]{:S(2)}, u32[]{:S(2)}) collective-permute-start(f32[64,1024]{1,0:T(8,128)S(1)} %bitcast.5), channel_id=1, source_target_pairs={{0,1},{1,0},{2,3},{3,2},{4,5},{5,4},{6,7},{7,6},{8,9},{9,8},{10,11... | collective-permute-start | bytes 786440 | tf_op jit(solution)/shard_map/ppermute | solution.py:307
  57.1 1.0 %copy-done = bf16[2,128,1024]{2,1,0:T(8,128)(2,1)S(1)} copy-done((bf16[2,128,1024]{2,1,0:T(8,128)(2,1)S(1)}, bf16[2,128,1024]{2,1,0:T(8,128)(2,1)}, u32[]{:S(2)}) %copy-start) | copy-done | bytes 524312
  58.2 1.0 %copy-done.1 = bf16[2,128,1024]{2,1,0:T(8,128)(2,1)S(1)} copy-done((bf16[2,128,1024]{2,1,0:T(8,128)(2,1)S(1)}, bf16[2,128,1024]{2,1,0:T(8,128)(2,1)}, u32[]{:S(2)}) %copy-start.1) | copy-done | bytes 524312
  59.2 1.0 %copy-done.5 = bf16[2,128,1024]{2,1,0:T(8,128)(2,1)S(1)} copy-done((bf16[2,128,1024]{2,1,0:T(8,128)(2,1)S(1)}, bf16[2,128,1024]{2,1,0:T(8,128)(2,1)}, u32[]{:S(2)}) %copy-start.5) | copy-done | bytes 524312
  60.2 1.0 %copy-done.7 = bf16[2,128,1024]{2,1,0:T(8,128)(2,1)S(1)} copy-done((bf16[2,128,1024]{2,1,0:T(8,128)(2,1)S(1)}, bf16[2,128,1024]{2,1,0:T(8,128)(2,1)}, u32[]{:S(2)}) %copy-start.7) | copy-done | bytes 524312
  61.3 0.7 copy-done.8
  62.0 3.5 %shard_map.70.begun_ref = f32[7,2,1024,128]{3,2,1,0:T(8,128)S(1)} custom-call(s32[2]{0:T(128)S(1)} %copy-done.8, bf16[2,128,1024]{2,1,0:T(8,128)(2,1)S(1)} %copy-done, bf16[2,128,1024]{2,1,0:T(8,128)(2,1)S(1)} %copy-done.1, bf16[2,128,1024]{2,1,0:T(8,128)(2,1)S(1)} %copy-done.5, bf16[2,128,1024]{2,1,0:T(8,128)(2,1)S(1)} %copy-done.7), custom_call_target="tpu_custom_call" | custom-call | flops 2097152000 | bytes 3145728 | tf_op jit(solution)/shard_map/pallas_call | solution.py:90
  65.5 0.0 copy-start.10
  65.5 0.0 copy-start.11
  65.5 3.3 %shard_map.71.slc_ref = f32[7,2,1024,128]{3,2,1,0:T(8,128)S(1)} custom-call(s32[2]{0:T(128)S(1)} %copy-done.8, bf16[2,128,1024]{2,1,0:T(8,128)(2,1)S(1)} %copy-done.3, bf16[2,128,1024]{2,1,0:T(8,128)(2,1)S(1)} %collective-permute-done.1.mate_phase, bf16[2,128,1024]{2,1,0:T(8,128)(2,1)S(1)} %collective-permute-done.4.via_amp, ...), custom_call_target="tpu_custom_call", output_to_operand_aliasing={{}: (6, {})} | custom-call | flops 2097152000 | bytes 3145728 | tf_op jit(solution)/shard_map/pallas_call | solution.py:90
  68.9 30.9 %shard_map.72 = (bf16[2,5,2,128,1024]{4,3,2,1,0:T(8,128)(2,1)}, bf16[2,5,128,1024]{3,2,1,0:T(8,128)(2,1)}) custom-call(s32[10]{0:T(128)S(1)} %reshape.11.slot_ref, s32[7]{0:T(128)S(1)} %compare_convert_fusion.valid_ref, s32[2]{0:T(128)S(1)} %copy-done.9, f32[7,2,1024,128]{3,2,1,0:T(8,128)S(1)} %shard_map.71.slc_ref, f32[64,1024]{1,0:T(8,128)S(1)} %bitcast.6, ...), custom_call_target="tpu_custom_call" | custom-call | flops 10000000000 | bytes 20000000 | tf_op jit(solution)/shard_map/pallas_call | solution.py:294
  (25 shorter events, 0.1 us)
Async XLA Ops:
  0.6 2.2 %collective-permute-start = (bf16[2,128,1024]{2,1,0:T(8,128)(2,1)}, bf16[2,128,1024]{2,1,0:T(8,128)(2,1)S(1)}, u32[]{:S(2)}, u32[]{:S(2)}) collective-permute-start(bf16[2,128,1024]{2,1,0:T(8,128)(2,1)} %own_amp.1), channel_id=1, source_target_pairs={{0,1},{1,0},{2,3},{3,2},{4,5},{5,4},{6,7},{7,6},{8,9},{9,8},{10,11... | collective-permute-start | bytes 1572872 | tf_op jit(solution)/shard_map/ppermute | solution.py:307
  2.8 0.8 copy-start.2
  6.0 59.5 %copy-start.3 = (bf16[2,128,1024]{2,1,0:T(8,128)(2,1)S(1)}, bf16[2,128,1024]{2,1,0:T(8,128)(2,1)}, u32[]{:S(2)}) copy-start(bf16[2,128,1024]{2,1,0:T(8,128)(2,1)} %copy-done.2) | copy-start | bytes 1572868
  6.0 20.2 %all-to-all-start = ((f32[8,2,8,1024]{3,2,1,0:T(8,128)}), f32[8,2,8,1024]{3,2,1,0:T(8,128)S(1)}, u32[]{:S(2)}, u32[]{:S(2)}) async-start(f32[8,2,8,1024]{3,2,1,0:T(8,128)} %get-tuple-element.6), calls=%async_computation | async-start | bytes 1048576 | tf_op jit(solution)/shard_map/all_to_all | solution.py:329
  12.8 24.0 %collective-permute-start.2 = (bf16[2,128,1024]{2,1,0:T(8,128)(2,1)}, bf16[2,128,1024]{2,1,0:T(8,128)(2,1)S(1)}, u32[]{:S(2)}, u32[]{:S(2)}) collective-permute-start(bf16[2,128,1024]{2,1,0:T(8,128)(2,1)} %own_amp.1), channel_id=1, source_target_pairs={{2,0},{3,1},{4,2},{5,3},{6,4},{7,5},{8,6},{9,7},{10,8},{11,9},{12,... | collective-permute-start | bytes 1572872 | tf_op jit(solution)/shard_map/ppermute | solution.py:307
  14.1 32.1 %collective-permute-start.3 = (bf16[2,128,1024]{2,1,0:T(8,128)(2,1)}, bf16[2,128,1024]{2,1,0:T(8,128)(2,1)S(1)}, u32[]{:S(2)}, u32[]{:S(2)}) collective-permute-start(bf16[2,128,1024]{2,1,0:T(8,128)(2,1)} %own_phase.1), channel_id=1, source_target_pairs={{2,0},{3,1},{4,2},{5,3},{6,4},{7,5},{8,6},{9,7},{10,8},{11,9},{12,... | collective-permute-start | bytes 1572872 | tf_op jit(solution)/shard_map/ppermute | solution.py:307
  27.0 28.3 %all-to-all-start.1 = ((f32[8,8,1024]{2,1,0:T(8,128)}), f32[8,8,1024]{2,1,0:T(8,128)S(1)}, u32[]{:S(2)}, u32[]{:S(2)}) async-start(f32[8,8,1024]{2,1,0:T(8,128)} %broadcast_in_dim.21.refs_2_), calls=%async_computation.1 | async-start | bytes 524288 | tf_op jit(solution)/shard_map/all_to_all | solution.py:335
  32.0 33.5 %collective-permute-start.1 = (bf16[2,128,1024]{2,1,0:T(8,128)(2,1)}, bf16[2,128,1024]{2,1,0:T(8,128)(2,1)S(1)}, u32[]{:S(2)}, u32[]{:S(2)}) collective-permute-start(bf16[2,128,1024]{2,1,0:T(8,128)(2,1)} %own_phase.1), channel_id=1, source_target_pairs={{1,0},{3,2},{5,4},{7,6},{9,8},{11,10},{13,12},{15,14},{17,16},{19,... | collective-permute-start | bytes 1572872 | tf_op jit(solution)/shard_map/ppermute | solution.py:307
  35.6 29.9 %collective-permute-start.6 = (bf16[2,128,1024]{2,1,0:T(8,128)(2,1)}, bf16[2,128,1024]{2,1,0:T(8,128)(2,1)S(1)}, u32[]{:S(2)}, u32[]{:S(2)}) collective-permute-start(bf16[2,128,1024]{2,1,0:T(8,128)(2,1)} %get-tuple-element.9), channel_id=1, source_target_pairs={{4,1},{6,3},{8,5},{10,7},{12,9},{14,11},{20,17},{22,19},{24,21},{2... | collective-permute-start | bytes 1572872 | tf_op jit(solution)/shard_map/ppermute | solution.py:307
  36.9 9.3 %copy-start.4 = (bf16[2,128,1024]{2,1,0:T(8,128)(2,1)}, bf16[2,128,1024]{2,1,0:T(8,128)(2,1)S(1)}, u32[]{:S(2)}) copy-start(bf16[2,128,1024]{2,1,0:T(8,128)(2,1)S(1)} %collective-permute-done.2.refs_0_) | copy-start | bytes 1572868
  46.2 0.8 copy-start.6
  47.0 18.5 %collective-permute-start.4 = (bf16[2,128,1024]{2,1,0:T(8,128)(2,1)}, bf16[2,128,1024]{2,1,0:T(8,128)(2,1)S(1)}, u32[]{:S(2)}, u32[]{:S(2)}) collective-permute-start(bf16[2,128,1024]{2,1,0:T(8,128)(2,1)} %get-tuple-element.7.next_amp), channel_id=1, source_target_pairs={{0,1},{1,0},{2,3},{3,2},{4,5},{5,4},{6,7},{7,6},{8,9},{9,8},{10,11... | collective-permute-start | bytes 1572872 | tf_op jit(solution)/shard_map/ppermute | solution.py:307
  47.7 17.8 %collective-permute-start.5 = (bf16[2,128,1024]{2,1,0:T(8,128)(2,1)}, bf16[2,128,1024]{2,1,0:T(8,128)(2,1)S(1)}, u32[]{:S(2)}, u32[]{:S(2)}) collective-permute-start(bf16[2,128,1024]{2,1,0:T(8,128)(2,1)} %get-tuple-element.8.next_phase), channel_id=1, source_target_pairs={{0,1},{1,0},{2,3},{3,2},{4,5},{5,4},{6,7},{7,6},{8,9},{9,8},{10,11... | collective-permute-start | bytes 1572872 | tf_op jit(solution)/shard_map/ppermute | solution.py:307
  55.3 13.5 %collective-permute-start.7 = (f32[64,1024]{1,0:T(8,128)S(1)}, f32[64,1024]{1,0:T(8,128)S(1)}, u32[]{:S(2)}, u32[]{:S(2)}) collective-permute-start(f32[64,1024]{1,0:T(8,128)S(1)} %bitcast.5), channel_id=1, source_target_pairs={{0,1},{1,0},{2,3},{3,2},{4,5},{5,4},{6,7},{7,6},{8,9},{9,8},{10,11... | collective-permute-start | bytes 786440 | tf_op jit(solution)/shard_map/ppermute | solution.py:307
  57.1 1.0 %copy-start = (bf16[2,128,1024]{2,1,0:T(8,128)(2,1)S(1)}, bf16[2,128,1024]{2,1,0:T(8,128)(2,1)}, u32[]{:S(2)}) copy-start(bf16[2,128,1024]{2,1,0:T(8,128)(2,1)} %own_amp.1) | copy-start | bytes 1572868
  58.2 1.0 %copy-start.1 = (bf16[2,128,1024]{2,1,0:T(8,128)(2,1)S(1)}, bf16[2,128,1024]{2,1,0:T(8,128)(2,1)}, u32[]{:S(2)}) copy-start(bf16[2,128,1024]{2,1,0:T(8,128)(2,1)} %own_phase.1) | copy-start | bytes 1572868
  59.2 1.0 %copy-start.5 = (bf16[2,128,1024]{2,1,0:T(8,128)(2,1)S(1)}, bf16[2,128,1024]{2,1,0:T(8,128)(2,1)}, u32[]{:S(2)}) copy-start(bf16[2,128,1024]{2,1,0:T(8,128)(2,1)} %get-tuple-element.7.next_amp) | copy-start | bytes 1572868
  60.2 1.0 %copy-start.7 = (bf16[2,128,1024]{2,1,0:T(8,128)(2,1)S(1)}, bf16[2,128,1024]{2,1,0:T(8,128)(2,1)}, u32[]{:S(2)}) copy-start(bf16[2,128,1024]{2,1,0:T(8,128)(2,1)} %get-tuple-element.8.next_phase) | copy-start | bytes 1572868
  61.3 0.7 copy-start.8
  65.5 3.4 %copy-start.9 = (s32[2]{0:T(128)S(1)}, s32[2]{0:T(128)}, u32[]{:S(2)}) copy-start(s32[2]{0:T(128)} %pad_add_fusion.place_ref) | copy-start | bytes 28
  65.5 3.4 %copy-start.10 = (s32[128,1024]{1,0:T(8,128)S(1)}, s32[128,1024]{1,0:T(8,128)}, u32[]{:S(2)}) copy-start(s32[128,1024]{1,0:T(8,128)} %half_ref.1) | copy-start | bytes 1572868
  65.5 3.4 %copy-start.11 = (bf16[3,128,256]{2,1,0:T(8,128)(2,1)S(1)}, bf16[3,128,256]{2,1,0:T(8,128)(2,1)}, u32[]{:S(2)}) copy-start(bf16[3,128,256]{2,1,0:T(8,128)(2,1)} %constant.43.clone.band_ref) | copy-start | bytes 589828

commit v2 on v1

--- a/solution.py
+++ b/solution.py
@@ -14,8 +14,8 @@
 CHUNK = 16
 PAD = 8
 
-SIN_TERMS = (1.0, -1.0 / 6, 1.0 / 120, -1.0 / 5040, 1.0 / 362880, -1.0 / 39916800, 1.0 / 6227020800)
-COS_TERMS = (1.0, -1.0 / 2, 1.0 / 24, -1.0 / 720, 1.0 / 40320, -1.0 / 3628800, 1.0 / 479001600)
+SIN_TERMS = (0.999999995714, -0.166666579612, 0.00833305031531, -0.000198090186189, 2.60509358011e-06)
+COS_TERMS = (0.99999999978, -0.499999993556, 0.0416666361503, -0.00138883600009, 2.47600883899e-05, -2.60501805941e-07)
 
 
 def series(square, terms):

time: 100 us -> 99.6 us (level)
  transfers between devices with their start and end apart: 10 -> 10, of which waited for: 4 -> 4; matrix products, arithmetic and copies ran while one was open for 2% -> 3% of each run, Pallas kernels for 7% -> 6%
where the time goes in v2:
time: 99.6 us; the launch traced here: 99 us
  Pallas kernels  39.3 us (39%)
  waiting for transfers between devices  28 us (28%)
  starting transfers between devices  21.9 us (22%)
  local copies, waits for them, and re-layouts  7.38 us (7%)
  other arithmetic  1.57 us (2%)
    pallas_call x1, Pallas kernels, interferograms(): pl.pallas_call(functools.partial(main_kernel, dates_dev), grid_spec=spec,...  30.9 us
    all_to_all x1, waiting for transfers between devices, local(): lax.all_to_all(pieces, 'date', 0, 0, axis_index_groups=groups)  10.7 us
    ppermute x8, waiting for transfers between devices, send(): return lax.ppermute(value, 'date', pairs)  10.7 us
    ppermute x8, starting transfers between devices, send(): return lax.ppermute(value, 'date', pairs)  10.1 us
    all_to_all x1, starting transfers between devices, local(): lax.all_to_all(pieces, 'date', 0, 0, axis_index_groups=groups)  6.82 us
    all_to_all x1, waiting for transfers between devices, local(): lax.all_to_all(copies, 'date', 0, 0, axis_index_groups=groups)  6.56 us
    unnamed x24, local copies, waits for them, and re-layouts  6.46 us
    pallas_call x2, Pallas kernels, slc_turned(): pl.pallas_call(kernel, in_specs=[SMEM] + [VMEM] * len(arrays), out_specs=...  5.99 us
  transfers between devices with their start and end apart: 10, of which 4 were waited for; matrix products, arithmetic and copies ran while one was open for 3% of the time, Pallas kernels for 6%

profile of v2, /device:TPU:1, one launch (start us, length us, event | category | flops | bytes accessed | tf_op | source)
XLA Modules:
  0.0 99.0 jit_solution(6972857494769204059)
XLA Ops:
  0.6 0.1 collective-permute-start
  0.8 0.7 pad_add_fusion.place_ref
  1.4 1.4 %collective-permute-done.mate_ref.mate_amp = bf16[2,128,1024]{2,1,0:T(8,128)(2,1)S(1)} collective-permute-done((bf16[2,128,1024]{2,1,0:T(8,128)(2,1)}, bf16[2,128,1024]{2,1,0:T(8,128)(2,1)S(1)}, u32[]{:S(2)}, u32[]{:S(2)}) %collective-permute-start) | collective-permute-done | bytes 524320 | tf_op jit(solution)/shard_map/ppermute | solution.py:307
  2.8 0.8 copy-done.2
  3.6 2.4 %shard_map.68 = (f32[8,2,8,1024]{3,2,1,0:T(8,128)}, bf16[2,128,1024]{2,1,0:T(8,128)(2,1)}) custom-call(s32[2]{0:T(128)} %pad_add_fusion.place_ref, bf16[2,128,1024]{2,1,0:T(8,128)(2,1)} %own_amp.1, bf16[2,128,1024]{2,1,0:T(8,128)(2,1)} %copy-done.2, bf16[2,128,1024]{2,1,0:T(8,128)(2,1)} %own_phase.1), custom_call_target="tpu_custom_call" | custom-call | flops 786432 | bytes 1572864 | tf_op jit(solution)/shard_map/pallas_call | solution.py:137
  6.0 6.8 %all-to-all-start = ((f32[8,2,8,1024]{3,2,1,0:T(8,128)}), f32[8,2,8,1024]{3,2,1,0:T(8,128)S(1)}, u32[]{:S(2)}, u32[]{:S(2)}) async-start(f32[8,2,8,1024]{3,2,1,0:T(8,128)} %get-tuple-element.6), calls=%async_computation | async-start | bytes 1048576 | tf_op jit(solution)/shard_map/all_to_all | solution.py:329
  12.8 1.3 %collective-permute-start.2 = (bf16[2,128,1024]{2,1,0:T(8,128)(2,1)}, bf16[2,128,1024]{2,1,0:T(8,128)(2,1)S(1)}, u32[]{:S(2)}, u32[]{:S(2)}) collective-permute-start(bf16[2,128,1024]{2,1,0:T(8,128)(2,1)} %own_amp.1), channel_id=1, source_target_pairs={{2,0},{3,1},{4,2},{5,3},{6,4},{7,5},{8,6},{9,7},{10,8},{11,9},{12,... | collective-permute-start | bytes 1572872 | tf_op jit(solution)/shard_map/ppermute | solution.py:307
  14.1 1.3 %collective-permute-start.3 = (bf16[2,128,1024]{2,1,0:T(8,128)(2,1)}, bf16[2,128,1024]{2,1,0:T(8,128)(2,1)S(1)}, u32[]{:S(2)}, u32[]{:S(2)}) collective-permute-start(bf16[2,128,1024]{2,1,0:T(8,128)(2,1)} %own_phase.1), channel_id=1, source_target_pairs={{2,0},{3,1},{4,2},{5,3},{6,4},{7,5},{8,6},{9,7},{10,8},{11,9},{12,... | collective-permute-start | bytes 1572872 | tf_op jit(solution)/shard_map/ppermute | solution.py:307
  15.4 10.7 %all-to-all-done = f32[8,2,8,1024]{3,2,1,0:T(8,128)S(1)} async-done(((f32[8,2,8,1024]{3,2,1,0:T(8,128)}), f32[8,2,8,1024]{3,2,1,0:T(8,128)S(1)}, u32[]{:S(2)}, u32[]{:S(2)}) %all-to-all-start) | async-done | bytes 524320 | tf_op jit(solution)/shard_map/all_to_all | solution.py:329
  26.2 0.7 broadcast_in_dim.21.refs_2_
  27.0 5.0 %all-to-all-start.1 = ((f32[8,8,1024]{2,1,0:T(8,128)}), f32[8,8,1024]{2,1,0:T(8,128)S(1)}, u32[]{:S(2)}, u32[]{:S(2)}) async-start(f32[8,8,1024]{2,1,0:T(8,128)} %broadcast_in_dim.21.refs_2_), calls=%async_computation.1 | async-start | bytes 524288 | tf_op jit(solution)/shard_map/all_to_all | solution.py:335
  32.0 3.6 %collective-permute-start.1 = (bf16[2,128,1024]{2,1,0:T(8,128)(2,1)}, bf16[2,128,1024]{2,1,0:T(8,128)(2,1)S(1)}, u32[]{:S(2)}, u32[]{:S(2)}) collective-permute-start(bf16[2,128,1024]{2,1,0:T(8,128)(2,1)} %own_phase.1), channel_id=1, source_target_pairs={{1,0},{3,2},{5,4},{7,6},{9,8},{11,10},{13,12},{15,14},{17,16},{19,... | collective-permute-start | bytes 1572872 | tf_op jit(solution)/shard_map/ppermute | solution.py:307
  35.6 1.3 %collective-permute-start.6 = (bf16[2,128,1024]{2,1,0:T(8,128)(2,1)}, bf16[2,128,1024]{2,1,0:T(8,128)(2,1)S(1)}, u32[]{:S(2)}, u32[]{:S(2)}) collective-permute-start(bf16[2,128,1024]{2,1,0:T(8,128)(2,1)} %get-tuple-element.9), channel_id=1, source_target_pairs={{4,1},{6,3},{8,5},{10,7},{12,9},{14,11},{20,17},{22,19},{24,21},{2... | collective-permute-start | bytes 1572872 | tf_op jit(solution)/shard_map/ppermute | solution.py:307
  36.9 0.0 copy-start.4
  36.9 9.3 %collective-permute-done.3.refs_1_ = bf16[2,128,1024]{2,1,0:T(8,128)(2,1)S(1)} collective-permute-done((bf16[2,128,1024]{2,1,0:T(8,128)(2,1)}, bf16[2,128,1024]{2,1,0:T(8,128)(2,1)S(1)}, u32[]{:S(2)}, u32[]{:S(2)}) %collective-permute-start.3) | collective-permute-done | bytes 524320 | tf_op jit(solution)/shard_map/ppermute | solution.py:307
  46.2 0.8 copy-done.6
  47.0 0.7 collective-permute-start.4
  47.7 0.8 fusion.6
  48.5 0.1 copy.10
  48.6 0.1 reshape.11.slot_ref
  48.7 6.6 %all-to-all-done.1 = f32[8,8,1024]{2,1,0:T(8,128)S(1)} async-done(((f32[8,8,1024]{2,1,0:T(8,128)}), f32[8,8,1024]{2,1,0:T(8,128)S(1)}, u32[]{:S(2)}, u32[]{:S(2)}) %all-to-all-start.1) | async-done | bytes 262176 | tf_op jit(solution)/shard_map/all_to_all | solution.py:335
  55.3 1.8 %collective-permute-start.7 = (f32[64,1024]{1,0:T(8,128)S(1)}, f32[64,1024]{1,0:T(8,128)S(1)}, u32[]{:S(2)}, u32[]{:S(2)}) collective-permute-start(f32[64,1024]{1,0:T(8,128)S(1)} %bitcast.5), channel_id=1, source_target_pairs={{0,1},{1,0},{2,3},{3,2},{4,5},{5,4},{6,7},{7,6},{8,9},{9,8},{10,11... | collective-permute-start | bytes 786440 | tf_op jit(solution)/shard_map/ppermute | solution.py:307
  57.1 1.0 %copy-done = bf16[2,128,1024]{2,1,0:T(8,128)(2,1)S(1)} copy-done((bf16[2,128,1024]{2,1,0:T(8,128)(2,1)S(1)}, bf16[2,128,1024]{2,1,0:T(8,128)(2,1)}, u32[]{:S(2)}) %copy-start) | copy-done | bytes 524312
  58.2 1.0 %copy-done.1 = bf16[2,128,1024]{2,1,0:T(8,128)(2,1)S(1)} copy-done((bf16[2,128,1024]{2,1,0:T(8,128)(2,1)S(1)}, bf16[2,128,1024]{2,1,0:T(8,128)(2,1)}, u32[]{:S(2)}) %copy-start.1) | copy-done | bytes 524312
  59.2 1.0 %copy-done.5 = bf16[2,128,1024]{2,1,0:T(8,128)(2,1)S(1)} copy-done((bf16[2,128,1024]{2,1,0:T(8,128)(2,1)S(1)}, bf16[2,128,1024]{2,1,0:T(8,128)(2,1)}, u32[]{:S(2)}) %copy-start.5) | copy-done | bytes 524312
  60.2 1.0 %copy-done.7 = bf16[2,128,1024]{2,1,0:T(8,128)(2,1)S(1)} copy-done((bf16[2,128,1024]{2,1,0:T(8,128)(2,1)S(1)}, bf16[2,128,1024]{2,1,0:T(8,128)(2,1)}, u32[]{:S(2)}) %copy-start.7) | copy-done | bytes 524312
  61.3 0.7 copy-done.8
  62.0 3.1 %shard_map.70.begun_ref = f32[7,2,1024,128]{3,2,1,0:T(8,128)S(1)} custom-call(s32[2]{0:T(128)S(1)} %copy-done.8, bf16[2,128,1024]{2,1,0:T(8,128)(2,1)S(1)} %copy-done, bf16[2,128,1024]{2,1,0:T(8,128)(2,1)S(1)} %copy-done.1, bf16[2,128,1024]{2,1,0:T(8,128)(2,1)S(1)} %copy-done.5, bf16[2,128,1024]{2,1,0:T(8,128)(2,1)S(1)} %copy-done.7), custom_call_target="tpu_custom_call" | custom-call | flops 2097152000 | bytes 3145728 | tf_op jit(solution)/shard_map/pallas_call | solution.py:90
  65.0 0.0 copy-start.10
  65.1 0.0 copy-start.11
  65.1 2.9 %shard_map.71.slc_ref = f32[7,2,1024,128]{3,2,1,0:T(8,128)S(1)} custom-call(s32[2]{0:T(128)S(1)} %copy-done.8, bf16[2,128,1024]{2,1,0:T(8,128)(2,1)S(1)} %copy-done.3, bf16[2,128,1024]{2,1,0:T(8,128)(2,1)S(1)} %collective-permute-done.1.mate_phase, bf16[2,128,1024]{2,1,0:T(8,128)(2,1)S(1)} %collective-permute-done.4.via_amp, ...), custom_call_target="tpu_custom_call", output_to_operand_aliasing={{}: (6, {})} | custom-call | flops 2097152000 | bytes 3145728 | tf_op jit(solution)/shard_map/pallas_call | solution.py:90
  68.1 30.9 %shard_map.72 = (bf16[2,5,2,128,1024]{4,3,2,1,0:T(8,128)(2,1)}, bf16[2,5,128,1024]{3,2,1,0:T(8,128)(2,1)}) custom-call(s32[10]{0:T(128)S(1)} %reshape.11.slot_ref, s32[7]{0:T(128)S(1)} %compare_convert_fusion.valid_ref, s32[2]{0:T(128)S(1)} %copy-done.9, f32[7,2,1024,128]{3,2,1,0:T(8,128)S(1)} %shard_map.71.slc_ref, f32[64,1024]{1,0:T(8,128)S(1)} %bitcast.6, ...), custom_call_target="tpu_custom_call" | custom-call | flops 10000000000 | bytes 20000000 | tf_op jit(solution)/shard_map/pallas_call | solution.py:294
  (25 shorter events, 0.1 us)
Async XLA Ops:
  0.6 2.2 %collective-permute-start = (bf16[2,128,1024]{2,1,0:T(8,128)(2,1)}, bf16[2,128,1024]{2,1,0:T(8,128)(2,1)S(1)}, u32[]{:S(2)}, u32[]{:S(2)}) collective-permute-start(bf16[2,128,1024]{2,1,0:T(8,128)(2,1)} %own_amp.1), channel_id=1, source_target_pairs={{0,1},{1,0},{2,3},{3,2},{4,5},{5,4},{6,7},{7,6},{8,9},{9,8},{10,11... | collective-permute-start | bytes 1572872 | tf_op jit(solution)/shard_map/ppermute | solution.py:307
  2.8 0.8 copy-start.2
  6.0 59.1 %copy-start.3 = (bf16[2,128,1024]{2,1,0:T(8,128)(2,1)S(1)}, bf16[2,128,1024]{2,1,0:T(8,128)(2,1)}, u32[]{:S(2)}) copy-start(bf16[2,128,1024]{2,1,0:T(8,128)(2,1)} %copy-done.2) | copy-start | bytes 1572868
  6.0 20.2 %all-to-all-start = ((f32[8,2,8,1024]{3,2,1,0:T(8,128)}), f32[8,2,8,1024]{3,2,1,0:T(8,128)S(1)}, u32[]{:S(2)}, u32[]{:S(2)}) async-start(f32[8,2,8,1024]{3,2,1,0:T(8,128)} %get-tuple-element.6), calls=%async_computation | async-start | bytes 1048576 | tf_op jit(solution)/shard_map/all_to_all | solution.py:329
  12.8 24.0 %collective-permute-start.2 = (bf16[2,128,1024]{2,1,0:T(8,128)(2,1)}, bf16[2,128,1024]{2,1,0:T(8,128)(2,1)S(1)}, u32[]{:S(2)}, u32[]{:S(2)}) collective-permute-start(bf16[2,128,1024]{2,1,0:T(8,128)(2,1)} %own_amp.1), channel_id=1, source_target_pairs={{2,0},{3,1},{4,2},{5,3},{6,4},{7,5},{8,6},{9,7},{10,8},{11,9},{12,... | collective-permute-start | bytes 1572872 | tf_op jit(solution)/shard_map/ppermute | solution.py:307
  14.1 32.1 %collective-permute-start.3 = (bf16[2,128,1024]{2,1,0:T(8,128)(2,1)}, bf16[2,128,1024]{2,1,0:T(8,128)(2,1)S(1)}, u32[]{:S(2)}, u32[]{:S(2)}) collective-permute-start(bf16[2,128,1024]{2,1,0:T(8,128)(2,1)} %own_phase.1), channel_id=1, source_target_pairs={{2,0},{3,1},{4,2},{5,3},{6,4},{7,5},{8,6},{9,7},{10,8},{11,9},{12,... | collective-permute-start | bytes 1572872 | tf_op jit(solution)/shard_map/ppermute | solution.py:307
  27.0 28.3 %all-to-all-start.1 = ((f32[8,8,1024]{2,1,0:T(8,128)}), f32[8,8,1024]{2,1,0:T(8,128)S(1)}, u32[]{:S(2)}, u32[]{:S(2)}) async-start(f32[8,8,1024]{2,1,0:T(8,128)} %broadcast_in_dim.21.refs_2_), calls=%async_computation.1 | async-start | bytes 524288 | tf_op jit(solution)/shard_map/all_to_all | solution.py:335
  32.0 33.1 %collective-permute-start.1 = (bf16[2,128,1024]{2,1,0:T(8,128)(2,1)}, bf16[2,128,1024]{2,1,0:T(8,128)(2,1)S(1)}, u32[]{:S(2)}, u32[]{:S(2)}) collective-permute-start(bf16[2,128,1024]{2,1,0:T(8,128)(2,1)} %own_phase.1), channel_id=1, source_target_pairs={{1,0},{3,2},{5,4},{7,6},{9,8},{11,10},{13,12},{15,14},{17,16},{19,... | collective-permute-start | bytes 1572872 | tf_op jit(solution)/shard_map/ppermute | solution.py:307
  35.6 29.5 %collective-permute-start.6 = (bf16[2,128,1024]{2,1,0:T(8,128)(2,1)}, bf16[2,128,1024]{2,1,0:T(8,128)(2,1)S(1)}, u32[]{:S(2)}, u32[]{:S(2)}) collective-permute-start(bf16[2,128,1024]{2,1,0:T(8,128)(2,1)} %get-tuple-element.9), channel_id=1, source_target_pairs={{4,1},{6,3},{8,5},{10,7},{12,9},{14,11},{20,17},{22,19},{24,21},{2... | collective-permute-start | bytes 1572872 | tf_op jit(solution)/shard_map/ppermute | solution.py:307
  36.9 9.3 %copy-start.4 = (bf16[2,128,1024]{2,1,0:T(8,128)(2,1)}, bf16[2,128,1024]{2,1,0:T(8,128)(2,1)S(1)}, u32[]{:S(2)}) copy-start(bf16[2,128,1024]{2,1,0:T(8,128)(2,1)S(1)} %collective-permute-done.2.refs_0_) | copy-start | bytes 1572868
  46.2 0.8 copy-start.6
  47.0 18.1 %collective-permute-start.4 = (bf16[2,128,1024]{2,1,0:T(8,128)(2,1)}, bf16[2,128,1024]{2,1,0:T(8,128)(2,1)S(1)}, u32[]{:S(2)}, u32[]{:S(2)}) collective-permute-start(bf16[2,128,1024]{2,1,0:T(8,128)(2,1)} %get-tuple-element.7.next_amp), channel_id=1, source_target_pairs={{0,1},{1,0},{2,3},{3,2},{4,5},{5,4},{6,7},{7,6},{8,9},{9,8},{10,11... | collective-permute-start | bytes 1572872 | tf_op jit(solution)/shard_map/ppermute | solution.py:307
  47.7 17.4 %collective-permute-start.5 = (bf16[2,128,1024]{2,1,0:T(8,128)(2,1)}, bf16[2,128,1024]{2,1,0:T(8,128)(2,1)S(1)}, u32[]{:S(2)}, u32[]{:S(2)}) collective-permute-start(bf16[2,128,1024]{2,1,0:T(8,128)(2,1)} %get-tuple-element.8.next_phase), channel_id=1, source_target_pairs={{0,1},{1,0},{2,3},{3,2},{4,5},{5,4},{6,7},{7,6},{8,9},{9,8},{10,11... | collective-permute-start | bytes 1572872 | tf_op jit(solution)/shard_map/ppermute | solution.py:307
  55.3 12.8 %collective-permute-start.7 = (f32[64,1024]{1,0:T(8,128)S(1)}, f32[64,1024]{1,0:T(8,128)S(1)}, u32[]{:S(2)}, u32[]{:S(2)}) collective-permute-start(f32[64,1024]{1,0:T(8,128)S(1)} %bitcast.5), channel_id=1, source_target_pairs={{0,1},{1,0},{2,3},{3,2},{4,5},{5,4},{6,7},{7,6},{8,9},{9,8},{10,11... | collective-permute-start | bytes 786440 | tf_op jit(solution)/shard_map/ppermute | solution.py:307
  57.1 1.0 %copy-start = (bf16[2,128,1024]{2,1,0:T(8,128)(2,1)S(1)}, bf16[2,128,1024]{2,1,0:T(8,128)(2,1)}, u32[]{:S(2)}) copy-start(bf16[2,128,1024]{2,1,0:T(8,128)(2,1)} %own_amp.1) | copy-start | bytes 1572868
  58.2 1.0 %copy-start.1 = (bf16[2,128,1024]{2,1,0:T(8,128)(2,1)S(1)}, bf16[2,128,1024]{2,1,0:T(8,128)(2,1)}, u32[]{:S(2)}) copy-start(bf16[2,128,1024]{2,1,0:T(8,128)(2,1)} %own_phase.1) | copy-start | bytes 1572868
  59.2 1.0 %copy-start.5 = (bf16[2,128,1024]{2,1,0:T(8,128)(2,1)S(1)}, bf16[2,128,1024]{2,1,0:T(8,128)(2,1)}, u32[]{:S(2)}) copy-start(bf16[2,128,1024]{2,1,0:T(8,128)(2,1)} %get-tuple-element.7.next_amp) | copy-start | bytes 1572868
  60.2 1.0 %copy-start.7 = (bf16[2,128,1024]{2,1,0:T(8,128)(2,1)S(1)}, bf16[2,128,1024]{2,1,0:T(8,128)(2,1)}, u32[]{:S(2)}) copy-start(bf16[2,128,1024]{2,1,0:T(8,128)(2,1)} %get-tuple-element.8.next_phase) | copy-start | bytes 1572868
  61.3 0.7 copy-start.8
  65.0 3.0 %copy-start.9 = (s32[2]{0:T(128)S(1)}, s32[2]{0:T(128)}, u32[]{:S(2)}) copy-start(s32[2]{0:T(128)} %pad_add_fusion.place_ref) | copy-start | bytes 28
  65.0 3.0 %copy-start.10 = (s32[128,1024]{1,0:T(8,128)S(1)}, s32[128,1024]{1,0:T(8,128)}, u32[]{:S(2)}) copy-start(s32[128,1024]{1,0:T(8,128)} %half_ref.1) | copy-start | bytes 1572868
  65.1 3.0 %copy-start.11 = (bf16[3,128,256]{2,1,0:T(8,128)(2,1)S(1)}, bf16[3,128,256]{2,1,0:T(8,128)(2,1)}, u32[]{:S(2)}) copy-start(bf16[3,128,256]{2,1,0:T(8,128)(2,1)} %constant.43.clone.band_ref) | copy-start | bytes 589828

commit v3 on v2

--- a/solution.py
+++ b/solution.py
@@ -51,8 +51,8 @@
 SMEM = pl.BlockSpec(memory_space=pltpu.SMEM)
 
 
-def slc_dates(place_ref, sources, slc_ref):
-    odd = place_ref[0] != 0
+def slc_dates(sources, slc_ref):
+    odd = lax.axis_index("date") % 2 != 0
 
     def body(n, carry):
         columns = pl.ds(pl.multiple_of(n * LANES, LANES), LANES)
@@ -69,33 +69,34 @@
     lax.fori_loop(0, sources[0][1][0].shape[2] // LANES, body, 0)
 
 
-def first_slc_kernel(place_ref, own_amp, own_phase, next_amp, next_phase, slc_ref):
-    own, following = (own_amp, own_phase), (next_amp, next_phase)
-    slc_dates(
-        place_ref,
-        [(0, own, 0, None, 0), (1, own, 1, None, 0), (4, following, 0, None, 0), (5, following, 1, None, 0)],
-        slc_ref,
-    )
-
-
-def second_slc_kernel(place_ref, mate_amp, mate_phase, via_amp, via_phase, last_ref, begun_ref, slc_ref):
-    mate, via, last = (mate_amp, mate_phase), (via_amp, via_phase), (last_ref.at[0:1], last_ref.at[1:2])
-    slc_dates(place_ref, [(2, via, 0, mate, 0), (3, via, 1, mate, 1), (6, last, 0, via, 0)], slc_ref)
-
-
-def slc_turned(kernel, place, *arrays, begun=None):
+def first_slc_kernel(next_amp, next_phase, slc_ref):
+    following = (next_amp, next_phase)
+    slc_dates([(4, following, 0, None, 0), (5, following, 1, None, 0)], slc_ref)
+
+
+def second_slc_kernel(
+    mate_amp, mate_phase, via_amp, via_phase, last_ref, own_amp, own_phase, begun_ref, slc_ref
+):
+    own, mate, via = (own_amp, own_phase), (mate_amp, mate_phase), (via_amp, via_phase)
+    last = (last_ref.at[0:1], last_ref.at[1:2])
+    sources = [(0, own, 0, None, 0), (1, own, 1, None, 0)]
+    sources += [(2, via, 0, mate, 0), (3, via, 1, mate, 1), (6, last, 0, via, 0)]
+    slc_dates(sources, slc_ref)
+
+
+def slc_turned(kernel, *arrays, begun=None):
     dates, rows, cols = arrays[0].shape
     if begun is not None:
         arrays = arrays + (begun,)
     return pl.pallas_call(
         kernel,
-        in_specs=[SMEM] + [VMEM] * len(arrays),
+        in_specs=[VMEM] * len(arrays),
         out_specs=VMEM,
         out_shape=jax.ShapeDtypeStruct((dates + REACH, 2, cols, rows), jnp.float32),
-        input_output_aliases={} if begun is None else {len(arrays): 0},
+        input_output_aliases={} if begun is None else {len(arrays) - 1: 0},
         compiler_params=pltpu.CompilerParams(vmem_limit_bytes=16 * 2**20),
         cost_estimate=cost(dates * rows * cols, 8000, 12),
-    )(place, *arrays)
+    )(*arrays)
 
 
 def gate_kernel(*refs):
@@ -336,8 +337,8 @@
     following = after(following, copies)
     via = [send(x, mate_pairs) for x in following]
     weights = (mine, send(mine, mate_pairs))
-    near = slc_turned(first_slc_kernel, place, amplitude, phase, *following)
-    slc = slc_turned(second_slc_kernel, place, amp_mate, phase_mate, *via, last, begun=near)
+    near = slc_turned(first_slc_kernel, *following)
+    slc = slc_turned(second_slc_kernel, amp_mate, phase_mate, *via, last, amplitude, phase, begun=near)
     valid = (index * dates_dev + jnp.arange(dates_dev + REACH) < total_dates).astype(jnp.int32)
     same = offset_code[:, None, :] == jnp.arange(REACH, dtype=jnp.int32)[None, :, None]
     slot = jnp.sum(jnp.where(same, jnp.arange(REACH, dtype=jnp.int32), 0), axis=2, dtype=jnp.int32).reshape(-1)

time: 99.6 us -> 96.9 us (0.973)
  local copies, waits for them, and re-layouts: 7.38 us -> 4.63 us
    unnamed x24 -> x22, local copies, waits for them, and re-layouts: 6.46 us -> 3.73 us
where the time goes in v3:
time: 96.9 us; the launch traced here: 96.4 us
  Pallas kernels  39.4 us (41%)
  waiting for transfers between devices  28.1 us (29%)
  starting transfers between devices  21.9 us (23%)
  local copies, waits for them, and re-layouts  4.63 us (5%)
  other arithmetic  1.54 us (2%)
    pallas_call x1, Pallas kernels, interferograms(): pl.pallas_call(functools.partial(main_kernel, dates_dev), grid_spec=spec,...  30.9 us
    ppermute x8, waiting for transfers between devices, send(): return lax.ppermute(value, 'date', pairs)  10.8 us
    all_to_all x1, waiting for transfers between devices, local(): lax.all_to_all(pieces, 'date', 0, 0, axis_index_groups=groups)  10.7 us
    ppermute x8, starting transfers between devices, send(): return lax.ppermute(value, 'date', pairs)  10.1 us
    all_to_all x1, starting transfers between devices, local(): lax.all_to_all(pieces, 'date', 0, 0, axis_index_groups=groups)  6.82 us
    all_to_all x1, waiting for transfers between devices, local(): lax.all_to_all(copies, 'date', 0, 0, axis_index_groups=groups)  6.54 us
    pallas_call x2, Pallas kernels, slc_turned(): pl.pallas_call(kernel, in_specs=[VMEM] * len(arrays), out_specs=VMEM, out...  6.12 us
    all_to_all x1, starting transfers between devices, local(): lax.all_to_all(copies, 'date', 0, 0, axis_index_groups=groups)  5.01 us
  transfers between devices with their start and end apart: 10, of which 4 were waited for; matrix products, arithmetic and copies ran while one was open for 3% of the time, Pallas kernels for 6%

profile of v3, /device:TPU:1, one launch (start us, length us, event | category | flops | bytes accessed | tf_op | source)
XLA Modules:
  0.0 96.4 jit_solution(8759788787228039068)
XLA Ops:
  0.6 0.0 copy-start
  0.6 0.0 copy-start.1
  0.7 0.1 collective-permute-start
  0.8 0.6 pad_add_fusion.place_ref
  1.4 1.4 %collective-permute-done.mate_ref.mate_amp = bf16[2,128,1024]{2,1,0:T(8,128)(2,1)S(1)} collective-permute-done((bf16[2,128,1024]{2,1,0:T(8,128)(2,1)}, bf16[2,128,1024]{2,1,0:T(8,128)(2,1)S(1)}, u32[]{:S(2)}, u32[]{:S(2)}) %collective-permute-start) | collective-permute-done | bytes 524320 | tf_op jit(solution)/shard_map/ppermute | solution.py:308
  2.8 0.8 copy-done.2
  3.6 2.4 %shard_map.68 = (f32[8,2,8,1024]{3,2,1,0:T(8,128)}, bf16[2,128,1024]{2,1,0:T(8,128)(2,1)}) custom-call(s32[2]{0:T(128)} %pad_add_fusion.place_ref, bf16[2,128,1024]{2,1,0:T(8,128)(2,1)} %own_amp.1, bf16[2,128,1024]{2,1,0:T(8,128)(2,1)} %copy-done.2, bf16[2,128,1024]{2,1,0:T(8,128)(2,1)} %own_phase.1), custom_call_target="tpu_custom_call" | custom-call | flops 786432 | bytes 1572864 | tf_op jit(solution)/shard_map/pallas_call | solution.py:138
  6.0 6.8 %all-to-all-start = ((f32[8,2,8,1024]{3,2,1,0:T(8,128)}), f32[8,2,8,1024]{3,2,1,0:T(8,128)S(1)}, u32[]{:S(2)}, u32[]{:S(2)}) async-start(f32[8,2,8,1024]{3,2,1,0:T(8,128)} %get-tuple-element.6), calls=%async_computation | async-start | bytes 1048576 | tf_op jit(solution)/shard_map/all_to_all | solution.py:330
  12.9 1.3 %collective-permute-start.2 = (bf16[2,128,1024]{2,1,0:T(8,128)(2,1)}, bf16[2,128,1024]{2,1,0:T(8,128)(2,1)S(1)}, u32[]{:S(2)}, u32[]{:S(2)}) collective-permute-start(bf16[2,128,1024]{2,1,0:T(8,128)(2,1)} %own_amp.1), channel_id=1, source_target_pairs={{2,0},{3,1},{4,2},{5,3},{6,4},{7,5},{8,6},{9,7},{10,8},{11,9},{12,... | collective-permute-start | bytes 1572872 | tf_op jit(solution)/shard_map/ppermute | solution.py:308
  14.2 1.3 %collective-permute-start.3 = (bf16[2,128,1024]{2,1,0:T(8,128)(2,1)}, bf16[2,128,1024]{2,1,0:T(8,128)(2,1)S(1)}, u32[]{:S(2)}, u32[]{:S(2)}) collective-permute-start(bf16[2,128,1024]{2,1,0:T(8,128)(2,1)} %own_phase.1), channel_id=1, source_target_pairs={{2,0},{3,1},{4,2},{5,3},{6,4},{7,5},{8,6},{9,7},{10,8},{11,9},{12,... | collective-permute-start | bytes 1572872 | tf_op jit(solution)/shard_map/ppermute | solution.py:308
  15.4 10.7 %all-to-all-done = f32[8,2,8,1024]{3,2,1,0:T(8,128)S(1)} async-done(((f32[8,2,8,1024]{3,2,1,0:T(8,128)}), f32[8,2,8,1024]{3,2,1,0:T(8,128)S(1)}, u32[]{:S(2)}, u32[]{:S(2)}) %all-to-all-start) | async-done | bytes 524320 | tf_op jit(solution)/shard_map/all_to_all | solution.py:330
  26.3 0.7 broadcast_in_dim.21.refs_2_
  27.0 5.0 %all-to-all-start.1 = ((f32[8,8,1024]{2,1,0:T(8,128)}), f32[8,8,1024]{2,1,0:T(8,128)S(1)}, u32[]{:S(2)}, u32[]{:S(2)}) async-start(f32[8,8,1024]{2,1,0:T(8,128)} %broadcast_in_dim.21.refs_2_), calls=%async_computation.1 | async-start | bytes 524288 | tf_op jit(solution)/shard_map/all_to_all | solution.py:336
  32.0 3.6 %collective-permute-start.1 = (bf16[2,128,1024]{2,1,0:T(8,128)(2,1)}, bf16[2,128,1024]{2,1,0:T(8,128)(2,1)S(1)}, u32[]{:S(2)}, u32[]{:S(2)}) collective-permute-start(bf16[2,128,1024]{2,1,0:T(8,128)(2,1)} %own_phase.1), channel_id=1, source_target_pairs={{1,0},{3,2},{5,4},{7,6},{9,8},{11,10},{13,12},{15,14},{17,16},{19,... | collective-permute-start | bytes 1572872 | tf_op jit(solution)/shard_map/ppermute | solution.py:308
  35.6 1.3 %collective-permute-start.6 = (bf16[2,128,1024]{2,1,0:T(8,128)(2,1)}, bf16[2,128,1024]{2,1,0:T(8,128)(2,1)}, u32[]{:S(2)}, u32[]{:S(2)}) collective-permute-start(bf16[2,128,1024]{2,1,0:T(8,128)(2,1)} %get-tuple-element.9), channel_id=1, source_target_pairs={{4,1},{6,3},{8,5},{10,7},{12,9},{14,11},{20,17},{22,19},{24,21},{2... | collective-permute-start | bytes 1572872 | tf_op jit(solution)/shard_map/ppermute | solution.py:308
  36.9 0.0 collective-permute-done.2.refs_0_
  36.9 0.0 copy-start.4
  36.9 9.3 %collective-permute-done.3.refs_1_ = bf16[2,128,1024]{2,1,0:T(8,128)(2,1)S(1)} collective-permute-done((bf16[2,128,1024]{2,1,0:T(8,128)(2,1)}, bf16[2,128,1024]{2,1,0:T(8,128)(2,1)S(1)}, u32[]{:S(2)}, u32[]{:S(2)}) %collective-permute-start.3) | collective-permute-done | bytes 524320 | tf_op jit(solution)/shard_map/ppermute | solution.py:308
  46.2 0.8 copy-done.6
  47.1 0.7 collective-permute-start.4
  47.7 0.8 fusion.6
  48.6 0.1 copy.10
  48.7 0.1 reshape.11.slot_ref
  48.8 6.5 %all-to-all-done.1 = f32[8,8,1024]{2,1,0:T(8,128)S(1)} async-done(((f32[8,8,1024]{2,1,0:T(8,128)}), f32[8,8,1024]{2,1,0:T(8,128)S(1)}, u32[]{:S(2)}, u32[]{:S(2)}) %all-to-all-start.1) | async-done | bytes 262176 | tf_op jit(solution)/shard_map/all_to_all | solution.py:336
  55.3 1.8 %collective-permute-start.7 = (f32[64,1024]{1,0:T(8,128)S(1)}, f32[64,1024]{1,0:T(8,128)S(1)}, u32[]{:S(2)}, u32[]{:S(2)}) collective-permute-start(f32[64,1024]{1,0:T(8,128)S(1)} %bitcast.5), channel_id=1, source_target_pairs={{0,1},{1,0},{2,3},{3,2},{4,5},{5,4},{6,7},{7,6},{8,9},{9,8},{10,11... | collective-permute-start | bytes 786440 | tf_op jit(solution)/shard_map/ppermute | solution.py:308
  57.1 1.0 %copy-done.5 = bf16[2,128,1024]{2,1,0:T(8,128)(2,1)S(1)} copy-done((bf16[2,128,1024]{2,1,0:T(8,128)(2,1)S(1)}, bf16[2,128,1024]{2,1,0:T(8,128)(2,1)}, u32[]{:S(2)}) %copy-start.5) | copy-done | bytes 524312
  58.2 1.0 %copy-done.7 = bf16[2,128,1024]{2,1,0:T(8,128)(2,1)S(1)} copy-done((bf16[2,128,1024]{2,1,0:T(8,128)(2,1)S(1)}, bf16[2,128,1024]{2,1,0:T(8,128)(2,1)}, u32[]{:S(2)}) %copy-start.7) | copy-done | bytes 524312
  59.2 1.6 %shard_map.70.begun_ref = f32[7,2,1024,128]{3,2,1,0:T(8,128)S(1)} custom-call(bf16[2,128,1024]{2,1,0:T(8,128)(2,1)S(1)} %copy-done.5, bf16[2,128,1024]{2,1,0:T(8,128)(2,1)S(1)} %copy-done.7), custom_call_target="tpu_custom_call" | custom-call | flops 2097152000 | bytes 3145728 | tf_op jit(solution)/shard_map/pallas_call | solution.py:91
  60.8 0.0 copy-start.9
  60.8 0.0 copy-start.10
  60.9 4.6 %shard_map.71.slc_ref = f32[7,2,1024,128]{3,2,1,0:T(8,128)S(1)} custom-call(bf16[2,128,1024]{2,1,0:T(8,128)(2,1)S(1)} %copy-done.3, bf16[2,128,1024]{2,1,0:T(8,128)(2,1)S(1)} %collective-permute-done.1.mate_phase, bf16[2,128,1024]{2,1,0:T(8,128)(2,1)S(1)} %collective-permute-done.4.via_amp, ...), custom_call_target="tpu_custom_call", output_to_operand_aliasing={{}: (7, {})} | custom-call | flops 2097152000 | bytes 3145728 | tf_op jit(solution)/shard_map/pallas_call | solution.py:91
  65.5 30.9 %shard_map.72 = (bf16[2,5,2,128,1024]{4,3,2,1,0:T(8,128)(2,1)}, bf16[2,5,128,1024]{3,2,1,0:T(8,128)(2,1)}) custom-call(s32[10]{0:T(128)S(1)} %reshape.11.slot_ref, s32[7]{0:T(128)S(1)} %compare_convert_fusion.valid_ref, s32[2]{0:T(128)S(1)} %copy-done.8, f32[7,2,1024,128]{3,2,1,0:T(8,128)S(1)} %shard_map.71.slc_ref, f32[64,1024]{1,0:T(8,128)S(1)} %bitcast.6, ...), custom_call_target="tpu_custom_call" | custom-call | flops 10000000000 | bytes 20000000 | tf_op jit(solution)/shard_map/pallas_call | solution.py:295
  (23 shorter events, 0.1 us)
Async XLA Ops:
  0.6 60.2 %copy-start = (bf16[2,128,1024]{2,1,0:T(8,128)(2,1)S(1)}, bf16[2,128,1024]{2,1,0:T(8,128)(2,1)}, u32[]{:S(2)}) copy-start(bf16[2,128,1024]{2,1,0:T(8,128)(2,1)} %own_amp.1) | copy-start | bytes 1572868
  0.6 60.2 %copy-start.1 = (bf16[2,128,1024]{2,1,0:T(8,128)(2,1)S(1)}, bf16[2,128,1024]{2,1,0:T(8,128)(2,1)}, u32[]{:S(2)}) copy-start(bf16[2,128,1024]{2,1,0:T(8,128)(2,1)} %own_phase.1) | copy-start | bytes 1572868
  0.7 2.2 %collective-permute-start = (bf16[2,128,1024]{2,1,0:T(8,128)(2,1)}, bf16[2,128,1024]{2,1,0:T(8,128)(2,1)S(1)}, u32[]{:S(2)}, u32[]{:S(2)}) collective-permute-start(bf16[2,128,1024]{2,1,0:T(8,128)(2,1)} %own_amp.1), channel_id=1, source_target_pairs={{0,1},{1,0},{2,3},{3,2},{4,5},{5,4},{6,7},{7,6},{8,9},{9,8},{10,11... | collective-permute-start | bytes 1572872 | tf_op jit(solution)/shard_map/ppermute | solution.py:308
  2.8 0.8 copy-start.2
  6.0 54.8 %copy-start.3 = (bf16[2,128,1024]{2,1,0:T(8,128)(2,1)S(1)}, bf16[2,128,1024]{2,1,0:T(8,128)(2,1)}, u32[]{:S(2)}) copy-start(bf16[2,128,1024]{2,1,0:T(8,128)(2,1)} %copy-done.2) | copy-start | bytes 1572868
  6.0 20.2 %all-to-all-start = ((f32[8,2,8,1024]{3,2,1,0:T(8,128)}), f32[8,2,8,1024]{3,2,1,0:T(8,128)S(1)}, u32[]{:S(2)}, u32[]{:S(2)}) async-start(f32[8,2,8,1024]{3,2,1,0:T(8,128)} %get-tuple-element.6), calls=%async_computation | async-start | bytes 1048576 | tf_op jit(solution)/shard_map/all_to_all | solution.py:330
  12.9 24.0 %collective-permute-start.2 = (bf16[2,128,1024]{2,1,0:T(8,128)(2,1)}, bf16[2,128,1024]{2,1,0:T(8,128)(2,1)S(1)}, u32[]{:S(2)}, u32[]{:S(2)}) collective-permute-start(bf16[2,128,1024]{2,1,0:T(8,128)(2,1)} %own_amp.1), channel_id=1, source_target_pairs={{2,0},{3,1},{4,2},{5,3},{6,4},{7,5},{8,6},{9,7},{10,8},{11,9},{12,... | collective-permute-start | bytes 1572872 | tf_op jit(solution)/shard_map/ppermute | solution.py:308
  14.2 32.1 %collective-permute-start.3 = (bf16[2,128,1024]{2,1,0:T(8,128)(2,1)}, bf16[2,128,1024]{2,1,0:T(8,128)(2,1)S(1)}, u32[]{:S(2)}, u32[]{:S(2)}) collective-permute-start(bf16[2,128,1024]{2,1,0:T(8,128)(2,1)} %own_phase.1), channel_id=1, source_target_pairs={{2,0},{3,1},{4,2},{5,3},{6,4},{7,5},{8,6},{9,7},{10,8},{11,9},{12,... | collective-permute-start | bytes 1572872 | tf_op jit(solution)/shard_map/ppermute | solution.py:308
  27.0 28.3 %all-to-all-start.1 = ((f32[8,8,1024]{2,1,0:T(8,128)}), f32[8,8,1024]{2,1,0:T(8,128)S(1)}, u32[]{:S(2)}, u32[]{:S(2)}) async-start(f32[8,8,1024]{2,1,0:T(8,128)} %broadcast_in_dim.21.refs_2_), calls=%async_computation.1 | async-start | bytes 524288 | tf_op jit(solution)/shard_map/all_to_all | solution.py:336
  32.0 28.8 %collective-permute-start.1 = (bf16[2,128,1024]{2,1,0:T(8,128)(2,1)}, bf16[2,128,1024]{2,1,0:T(8,128)(2,1)S(1)}, u32[]{:S(2)}, u32[]{:S(2)}) collective-permute-start(bf16[2,128,1024]{2,1,0:T(8,128)(2,1)} %own_phase.1), channel_id=1, source_target_pairs={{1,0},{3,2},{5,4},{7,6},{9,8},{11,10},{13,12},{15,14},{17,16},{19,... | collective-permute-start | bytes 1572872 | tf_op jit(solution)/shard_map/ppermute | solution.py:308
  35.6 25.3 %collective-permute-start.6 = (bf16[2,128,1024]{2,1,0:T(8,128)(2,1)}, bf16[2,128,1024]{2,1,0:T(8,128)(2,1)}, u32[]{:S(2)}, u32[]{:S(2)}) collective-permute-start(bf16[2,128,1024]{2,1,0:T(8,128)(2,1)} %get-tuple-element.9), channel_id=1, source_target_pairs={{4,1},{6,3},{8,5},{10,7},{12,9},{14,11},{20,17},{22,19},{24,21},{2... | collective-permute-start | bytes 1572872 | tf_op jit(solution)/shard_map/ppermute | solution.py:308
  36.9 9.3 %copy-start.4 = (bf16[2,128,1024]{2,1,0:T(8,128)(2,1)}, bf16[2,128,1024]{2,1,0:T(8,128)(2,1)S(1)}, u32[]{:S(2)}) copy-start(bf16[2,128,1024]{2,1,0:T(8,128)(2,1)S(1)} %collective-permute-done.2.refs_0_) | copy-start | bytes 1572868
  46.2 0.8 copy-start.6
  47.1 13.8 %collective-permute-start.4 = (bf16[2,128,1024]{2,1,0:T(8,128)(2,1)}, bf16[2,128,1024]{2,1,0:T(8,128)(2,1)S(1)}, u32[]{:S(2)}, u32[]{:S(2)}) collective-permute-start(bf16[2,128,1024]{2,1,0:T(8,128)(2,1)} %get-tuple-element.7.next_amp), channel_id=1, source_target_pairs={{0,1},{1,0},{2,3},{3,2},{4,5},{5,4},{6,7},{7,6},{8,9},{9,8},{10,11... | collective-permute-start | bytes 1572872 | tf_op jit(solution)/shard_map/ppermute | solution.py:308
  47.7 13.1 %collective-permute-start.5 = (bf16[2,128,1024]{2,1,0:T(8,128)(2,1)}, bf16[2,128,1024]{2,1,0:T(8,128)(2,1)S(1)}, u32[]{:S(2)}, u32[]{:S(2)}) collective-permute-start(bf16[2,128,1024]{2,1,0:T(8,128)(2,1)} %get-tuple-element.8.next_phase), channel_id=1, source_target_pairs={{0,1},{1,0},{2,3},{3,2},{4,5},{5,4},{6,7},{7,6},{8,9},{9,8},{10,11... | collective-permute-start | bytes 1572872 | tf_op jit(solution)/shard_map/ppermute | solution.py:308
  55.3 10.1 %collective-permute-start.7 = (f32[64,1024]{1,0:T(8,128)S(1)}, f32[64,1024]{1,0:T(8,128)S(1)}, u32[]{:S(2)}, u32[]{:S(2)}) collective-permute-start(f32[64,1024]{1,0:T(8,128)S(1)} %bitcast.5), channel_id=1, source_target_pairs={{0,1},{1,0},{2,3},{3,2},{4,5},{5,4},{6,7},{7,6},{8,9},{9,8},{10,11... | collective-permute-start | bytes 786440 | tf_op jit(solution)/shard_map/ppermute | solution.py:308
  57.1 1.0 %copy-start.5 = (bf16[2,128,1024]{2,1,0:T(8,128)(2,1)S(1)}, bf16[2,128,1024]{2,1,0:T(8,128)(2,1)}, u32[]{:S(2)}) copy-start(bf16[2,128,1024]{2,1,0:T(8,128)(2,1)} %get-tuple-element.7.next_amp) | copy-start | bytes 1572868
  58.2 1.0 %copy-start.7 = (bf16[2,128,1024]{2,1,0:T(8,128)(2,1)S(1)}, bf16[2,128,1024]{2,1,0:T(8,128)(2,1)}, u32[]{:S(2)}) copy-start(bf16[2,128,1024]{2,1,0:T(8,128)(2,1)} %get-tuple-element.8.next_phase) | copy-start | bytes 1572868
  60.8 4.7 %copy-start.8 = (s32[2]{0:T(128)S(1)}, s32[2]{0:T(128)}, u32[]{:S(2)}) copy-start(s32[2]{0:T(128)} %pad_add_fusion.place_ref) | copy-start | bytes 28
  60.8 4.7 %copy-start.9 = (s32[128,1024]{1,0:T(8,128)S(1)}, s32[128,1024]{1,0:T(8,128)}, u32[]{:S(2)}) copy-start(s32[128,1024]{1,0:T(8,128)} %half_ref.1) | copy-start | bytes 1572868
  60.8 4.7 %copy-start.10 = (bf16[3,128,256]{2,1,0:T(8,128)(2,1)S(1)}, bf16[3,128,256]{2,1,0:T(8,128)(2,1)}, u32[]{:S(2)}) copy-start(bf16[3,128,256]{2,1,0:T(8,128)(2,1)} %constant.43.clone.band_ref) | copy-start | bytes 589828

commit v4 on v3

--- a/solution.py
+++ b/solution.py
@@ -328,13 +328,14 @@
     amp_mate = send(amplitude, mate_pairs)
     pieces, early = moment_pieces(place, amplitude, amp_mate, phase, chips)
     moments = jnp.sum(lax.all_to_all(pieces, "date", 0, 0, axis_index_groups=groups), axis=0)
-    following = [send(x, next_pairs) for x in (amplitude, phase)]
+    following = [send(amplitude, next_pairs)]
     last = send(early, last_pairs)
     phase_mate = send(phase, to_even)
     weight = spread_weight(moments[0], moments[1], total_dates)
     copies = jnp.broadcast_to(weight[None], (chips,) + weight.shape)
     mine = lax.all_to_all(copies, "date", 0, 0, axis_index_groups=groups).reshape(rows // 2, cols)
-    following = after(following, copies)
+    (late,) = after([phase], copies)
+    following = [*after(following, copies), send(late, next_pairs)]
     via = [send(x, mate_pairs) for x in following]
     weights = (mine, send(mine, mate_pairs))
     near = slc_turned(first_slc_kernel, *following)

time: 96.9 us -> 96.5 us (level)
  waiting for transfers between devices: 28.1 us -> 23.9 us
  starting transfers between devices: 21.9 us -> 25 us
    ppermute x8, waiting for transfers between devices: 10.8 us -> 5.88 us  [send(): return lax.ppermute(value, 'date', pairs)]
    ppermute x8, starting transfers between devices: 10.1 us -> 12.8 us  [send(): return lax.ppermute(value, 'date', pairs)]
    all_to_all x1, waiting for transfers between devices: 6.54 us -> 7.83 us  [local(): lax.all_to_all(copies, 'date', 0, 0, axis_index_groups=groups)]
    unnamed x22 -> x21, local copies, waits for them, and re-layouts: 3.73 us -> 4.55 us
  transfers between devices with their start and end apart: 10 -> 10, of which waited for: 4 -> 4; matrix products, arithmetic and copies ran while one was open for 3% -> 4% of each run, Pallas kernels for 6% -> 7%
where the time goes in v4:
time: 96.5 us; the launch traced here: 95.5 us
  Pallas kernels  39.5 us (41%)
  starting transfers between devices  25 us (26%)
  waiting for transfers between devices  23.9 us (25%)
  local copies, waits for them, and re-layouts  5.45 us (6%)
    pallas_call x1, Pallas kernels, interferograms(): pl.pallas_call(functools.partial(main_kernel, dates_dev), grid_spec=spec,...  30.9 us
    ppermute x8, starting transfers between devices, send(): return lax.ppermute(value, 'date', pairs)  12.8 us
    all_to_all x1, waiting for transfers between devices, local(): lax.all_to_all(pieces, 'date', 0, 0, axis_index_groups=groups)  10.2 us
    all_to_all x1, waiting for transfers between devices, local(): lax.all_to_all(copies, 'date', 0, 0, axis_index_groups=groups)  7.83 us
    all_to_all x1, starting transfers between devices, local(): lax.all_to_all(pieces, 'date', 0, 0, axis_index_groups=groups)  6.83 us
    pallas_call x2, Pallas kernels, slc_turned(): pl.pallas_call(kernel, in_specs=[VMEM] * len(arrays), out_specs=VMEM, out...  6.26 us
    ppermute x8, waiting for transfers between devices, send(): return lax.ppermute(value, 'date', pairs)  5.88 us
    all_to_all x1, starting transfers between devices, local(): lax.all_to_all(copies, 'date', 0, 0, axis_index_groups=groups)  5.32 us
  transfers between devices with their start and end apart: 10, of which 4 were waited for; matrix products, arithmetic and copies ran while one was open for 4% of the time, Pallas kernels for 7%

profile of v4, /device:TPU:1, one launch (start us, length us, event | category | flops | bytes accessed | tf_op | source)
XLA Modules:
  0.0 95.5 jit_solution(15753502693978879264)
XLA Ops:
  0.6 0.1 collective-permute-start
  0.8 0.6 pad_add_fusion.place_ref
  1.4 1.5 %collective-permute-done.mate_ref.mate_amp = bf16[2,128,1024]{2,1,0:T(8,128)(2,1)S(1)} collective-permute-done((bf16[2,128,1024]{2,1,0:T(8,128)(2,1)}, bf16[2,128,1024]{2,1,0:T(8,128)(2,1)S(1)}, u32[]{:S(2)}, u32[]{:S(2)}) %collective-permute-start) | collective-permute-done | bytes 524320 | tf_op jit(solution)/shard_map/ppermute | solution.py:308
  2.8 0.8 copy-done.2
  3.6 2.4 %shard_map.68 = (f32[8,2,8,1024]{3,2,1,0:T(8,128)}, bf16[2,128,1024]{2,1,0:T(8,128)(2,1)}) custom-call(s32[2]{0:T(128)} %pad_add_fusion.place_ref, bf16[2,128,1024]{2,1,0:T(8,128)(2,1)} %own_amp.1, bf16[2,128,1024]{2,1,0:T(8,128)(2,1)} %copy-done.2, bf16[2,128,1024]{2,1,0:T(8,128)(2,1)} %own_phase.1), custom_call_target="tpu_custom_call" | custom-call | flops 786432 | bytes 1572864 | tf_op jit(solution)/shard_map/pallas_call | solution.py:138
  6.0 6.8 %all-to-all-start = ((f32[8,2,8,1024]{3,2,1,0:T(8,128)}), f32[8,2,8,1024]{3,2,1,0:T(8,128)S(1)}, u32[]{:S(2)}, u32[]{:S(2)}) async-start(f32[8,2,8,1024]{3,2,1,0:T(8,128)} %get-tuple-element.4), calls=%async_computation | async-start | bytes 1048576 | tf_op jit(solution)/shard_map/all_to_all | solution.py:330
  12.9 1.3 %collective-permute-start.2 = (bf16[2,128,1024]{2,1,0:T(8,128)(2,1)}, bf16[2,128,1024]{2,1,0:T(8,128)(2,1)S(1)}, u32[]{:S(2)}, u32[]{:S(2)}) collective-permute-start(bf16[2,128,1024]{2,1,0:T(8,128)(2,1)} %own_amp.1), channel_id=1, source_target_pairs={{2,0},{3,1},{4,2},{5,3},{6,4},{7,5},{8,6},{9,7},{10,8},{11,9},{12,... | collective-permute-start | bytes 1572872 | tf_op jit(solution)/shard_map/ppermute | solution.py:308
  14.2 1.9 %copy.12.refs_0_ = bf16[2,128,1024]{2,1,0:T(8,128)(2,1)} copy(bf16[2,128,1024]{2,1,0:T(8,128)(2,1)} %own_phase.1) | data formatting | bytes 1048576
  16.1 10.2 %all-to-all-done = f32[8,2,8,1024]{3,2,1,0:T(8,128)S(1)} async-done(((f32[8,2,8,1024]{3,2,1,0:T(8,128)}), f32[8,2,8,1024]{3,2,1,0:T(8,128)S(1)}, u32[]{:S(2)}, u32[]{:S(2)}) %all-to-all-start) | async-done | bytes 524320 | tf_op jit(solution)/shard_map/all_to_all | solution.py:330
  26.3 0.7 broadcast_in_dim.21.refs_1_
  27.0 1.3 %collective-permute-start.4 = (bf16[2,128,1024]{2,1,0:T(8,128)(2,1)}, bf16[2,128,1024]{2,1,0:T(8,128)(2,1)S(1)}, u32[]{:S(2)}, u32[]{:S(2)}) collective-permute-start(bf16[2,128,1024]{2,1,0:T(8,128)(2,1)} %shard_map.70), channel_id=1, source_target_pairs={{2,0},{3,1},{4,2},{5,3},{6,4},{7,5},{8,6},{9,7},{10,8},{11,9},{12,... | collective-permute-start | bytes 1572872 | tf_op jit(solution)/shard_map/ppermute | solution.py:308
  28.3 5.3 %all-to-all-start.1 = ((f32[8,8,1024]{2,1,0:T(8,128)}), f32[8,8,1024]{2,1,0:T(8,128)S(1)}, u32[]{:S(2)}, u32[]{:S(2)}) async-start(f32[8,8,1024]{2,1,0:T(8,128)} %broadcast_in_dim.21.refs_1_), calls=%async_computation.1 | async-start | bytes 524288 | tf_op jit(solution)/shard_map/all_to_all | solution.py:336
  33.6 3.8 %collective-permute-start.1 = (bf16[2,128,1024]{2,1,0:T(8,128)(2,1)}, bf16[2,128,1024]{2,1,0:T(8,128)(2,1)S(1)}, u32[]{:S(2)}, u32[]{:S(2)}) collective-permute-start(bf16[2,128,1024]{2,1,0:T(8,128)(2,1)} %own_phase.1), channel_id=1, source_target_pairs={{1,0},{3,2},{5,4},{7,6},{9,8},{11,10},{13,12},{15,14},{17,16},{19,... | collective-permute-start | bytes 1572872 | tf_op jit(solution)/shard_map/ppermute | solution.py:308
  37.4 1.3 %collective-permute-start.6 = (bf16[2,128,1024]{2,1,0:T(8,128)(2,1)}, bf16[2,128,1024]{2,1,0:T(8,128)(2,1)}, u32[]{:S(2)}, u32[]{:S(2)}) collective-permute-start(bf16[2,128,1024]{2,1,0:T(8,128)(2,1)} %get-tuple-element.5), channel_id=1, source_target_pairs={{4,1},{6,3},{8,5},{10,7},{12,9},{14,11},{20,17},{22,19},{24,21},{2... | collective-permute-start | bytes 1572872 | tf_op jit(solution)/shard_map/ppermute | solution.py:308
  38.7 0.0 collective-permute-done.2.refs_0_
  38.7 0.0 copy-start.4
  38.7 0.8 copy-done.4
  39.5 0.0 collective-permute-start.3
  39.5 4.4 %collective-permute-done.4.next_phase = bf16[2,128,1024]{2,1,0:T(8,128)(2,1)S(1)} collective-permute-done((bf16[2,128,1024]{2,1,0:T(8,128)(2,1)}, bf16[2,128,1024]{2,1,0:T(8,128)(2,1)S(1)}, u32[]{:S(2)}, u32[]{:S(2)}) %collective-permute-start.4) | collective-permute-done | bytes 524320 | tf_op jit(solution)/shard_map/ppermute | solution.py:308
  43.9 3.3 %collective-permute-start.5 = (bf16[2,128,1024]{2,1,0:T(8,128)(2,1)S(1)}, bf16[2,128,1024]{2,1,0:T(8,128)(2,1)}, u32[]{:S(2)}, u32[]{:S(2)}) collective-permute-start(bf16[2,128,1024]{2,1,0:T(8,128)(2,1)S(1)} %collective-permute-done.4.next_phase), channel_id=1, source_target_pairs={{0,1},{1,0},{2,3},{3,2},{4,5},{5,4},{6,7},{7,6},{8,9},{9,8},{10,11... | collective-permute-start | bytes 1572872 | tf_op jit(solution)/shard_map/ppermute | solution.py:308
  47.1 0.2 fusion.6
  47.3 0.1 copy.10
  47.4 0.1 reshape.11.slot_ref
  47.5 7.8 %all-to-all-done.1 = f32[8,8,1024]{2,1,0:T(8,128)S(1)} async-done(((f32[8,8,1024]{2,1,0:T(8,128)}), f32[8,8,1024]{2,1,0:T(8,128)S(1)}, u32[]{:S(2)}, u32[]{:S(2)}) %all-to-all-start.1) | async-done | bytes 262176 | tf_op jit(solution)/shard_map/all_to_all | solution.py:336
  55.3 1.8 %collective-permute-start.7 = (f32[64,1024]{1,0:T(8,128)S(1)}, f32[64,1024]{1,0:T(8,128)S(1)}, u32[]{:S(2)}, u32[]{:S(2)}) collective-permute-start(f32[64,1024]{1,0:T(8,128)S(1)} %bitcast.5), channel_id=1, source_target_pairs={{0,1},{1,0},{2,3},{3,2},{4,5},{5,4},{6,7},{7,6},{8,9},{9,8},{10,11... | collective-permute-start | bytes 786440 | tf_op jit(solution)/shard_map/ppermute | solution.py:308
  57.1 1.0 %copy-done.5 = bf16[2,128,1024]{2,1,0:T(8,128)(2,1)S(1)} copy-done((bf16[2,128,1024]{2,1,0:T(8,128)(2,1)S(1)}, bf16[2,128,1024]{2,1,0:T(8,128)(2,1)}, u32[]{:S(2)}) %copy-start.5) | copy-done | bytes 524312
  58.2 1.6 %shard_map.71.begun_ref = f32[7,2,1024,128]{3,2,1,0:T(8,128)S(1)} custom-call(bf16[2,128,1024]{2,1,0:T(8,128)(2,1)S(1)} %copy-done.5, bf16[2,128,1024]{2,1,0:T(8,128)(2,1)S(1)} %collective-permute-done.4.next_phase), custom_call_target="tpu_custom_call" | custom-call | flops 2097152000 | bytes 3145728 | tf_op jit(solution)/shard_map/pallas_call | solution.py:91
  59.8 0.0 copy-start.7
  59.8 0.0 copy-start.8
  59.8 0.0 collective-permute-done.1.mate_phase
  59.9 4.7 %shard_map.72.slc_ref = f32[7,2,1024,128]{3,2,1,0:T(8,128)S(1)} custom-call(bf16[2,128,1024]{2,1,0:T(8,128)(2,1)S(1)} %copy-done.3, bf16[2,128,1024]{2,1,0:T(8,128)(2,1)S(1)} %collective-permute-done.1.mate_phase, bf16[2,128,1024]{2,1,0:T(8,128)(2,1)S(1)} %collective-permute-done.3.via_amp, ...), custom_call_target="tpu_custom_call", output_to_operand_aliasing={{}: (7, {})} | custom-call | flops 2097152000 | bytes 3145728 | tf_op jit(solution)/shard_map/pallas_call | solution.py:91
  64.6 30.9 %shard_map.73 = (bf16[2,5,2,128,1024]{4,3,2,1,0:T(8,128)(2,1)}, bf16[2,5,128,1024]{3,2,1,0:T(8,128)(2,1)}) custom-call(s32[10]{0:T(128)S(1)} %reshape.11.slot_ref, s32[7]{0:T(128)S(1)} %compare_convert_fusion.valid_ref, s32[2]{0:T(128)S(1)} %copy-done.6, f32[7,2,1024,128]{3,2,1,0:T(8,128)S(1)} %shard_map.72.slc_ref, f32[64,1024]{1,0:T(8,128)S(1)} %bitcast.6, ...), custom_call_target="tpu_custom_call" | custom-call | flops 10000000000 | bytes 20000000 | tf_op jit(solution)/shard_map/pallas_call | solution.py:295
  (23 shorter events, 0.1 us)
Async XLA Ops:
  0.6 46.5 %copy-start.9 = (s32[2,5]{1,0:T(2,128)S(1)}, s32[2,5]{1,0:T(2,128)}, u32[]{:S(2)}) copy-start(s32[2,5]{1,0:T(2,128)} %param.7) | copy-start | bytes 124
  0.6 2.2 %collective-permute-start = (bf16[2,128,1024]{2,1,0:T(8,128)(2,1)}, bf16[2,128,1024]{2,1,0:T(8,128)(2,1)S(1)}, u32[]{:S(2)}, u32[]{:S(2)}) collective-permute-start(bf16[2,128,1024]{2,1,0:T(8,128)(2,1)} %own_amp.1), channel_id=1, source_target_pairs={{0,1},{1,0},{2,3},{3,2},{4,5},{5,4},{6,7},{7,6},{8,9},{9,8},{10,11... | collective-permute-start | bytes 1572872 | tf_op jit(solution)/shard_map/ppermute | solution.py:308
  2.8 0.8 copy-start.2
  6.0 53.8 %copy-start = (bf16[2,128,1024]{2,1,0:T(8,128)(2,1)S(1)}, bf16[2,128,1024]{2,1,0:T(8,128)(2,1)}, u32[]{:S(2)}) copy-start(bf16[2,128,1024]{2,1,0:T(8,128)(2,1)} %own_phase.1) | copy-start | bytes 1572868
  6.0 53.8 %copy-start.1 = (bf16[2,128,1024]{2,1,0:T(8,128)(2,1)S(1)}, bf16[2,128,1024]{2,1,0:T(8,128)(2,1)}, u32[]{:S(2)}) copy-start(bf16[2,128,1024]{2,1,0:T(8,128)(2,1)} %own_amp.1) | copy-start | bytes 1572868
  6.0 53.8 %copy-start.3 = (bf16[2,128,1024]{2,1,0:T(8,128)(2,1)S(1)}, bf16[2,128,1024]{2,1,0:T(8,128)(2,1)}, u32[]{:S(2)}) copy-start(bf16[2,128,1024]{2,1,0:T(8,128)(2,1)} %copy-done.2) | copy-start | bytes 1572868
  6.0 20.2 %all-to-all-start = ((f32[8,2,8,1024]{3,2,1,0:T(8,128)}), f32[8,2,8,1024]{3,2,1,0:T(8,128)S(1)}, u32[]{:S(2)}, u32[]{:S(2)}) async-start(f32[8,2,8,1024]{3,2,1,0:T(8,128)} %get-tuple-element.4), calls=%async_computation | async-start | bytes 1048576 | tf_op jit(solution)/shard_map/all_to_all | solution.py:330
  12.9 25.8 %collective-permute-start.2 = (bf16[2,128,1024]{2,1,0:T(8,128)(2,1)}, bf16[2,128,1024]{2,1,0:T(8,128)(2,1)S(1)}, u32[]{:S(2)}, u32[]{:S(2)}) collective-permute-start(bf16[2,128,1024]{2,1,0:T(8,128)(2,1)} %own_amp.1), channel_id=1, source_target_pairs={{2,0},{3,1},{4,2},{5,3},{6,4},{7,5},{8,6},{9,7},{10,8},{11,9},{12,... | collective-permute-start | bytes 1572872 | tf_op jit(solution)/shard_map/ppermute | solution.py:308
  27.0 16.9 %collective-permute-start.4 = (bf16[2,128,1024]{2,1,0:T(8,128)(2,1)}, bf16[2,128,1024]{2,1,0:T(8,128)(2,1)S(1)}, u32[]{:S(2)}, u32[]{:S(2)}) collective-permute-start(bf16[2,128,1024]{2,1,0:T(8,128)(2,1)} %shard_map.70), channel_id=1, source_target_pairs={{2,0},{3,1},{4,2},{5,3},{6,4},{7,5},{8,6},{9,7},{10,8},{11,9},{12,... | collective-permute-start | bytes 1572872 | tf_op jit(solution)/shard_map/ppermute | solution.py:308
  28.3 27.1 %all-to-all-start.1 = ((f32[8,8,1024]{2,1,0:T(8,128)}), f32[8,8,1024]{2,1,0:T(8,128)S(1)}, u32[]{:S(2)}, u32[]{:S(2)}) async-start(f32[8,8,1024]{2,1,0:T(8,128)} %broadcast_in_dim.21.refs_1_), calls=%async_computation.1 | async-start | bytes 524288 | tf_op jit(solution)/shard_map/all_to_all | solution.py:336
  33.6 26.2 %collective-permute-start.1 = (bf16[2,128,1024]{2,1,0:T(8,128)(2,1)}, bf16[2,128,1024]{2,1,0:T(8,128)(2,1)S(1)}, u32[]{:S(2)}, u32[]{:S(2)}) collective-permute-start(bf16[2,128,1024]{2,1,0:T(8,128)(2,1)} %own_phase.1), channel_id=1, source_target_pairs={{1,0},{3,2},{5,4},{7,6},{9,8},{11,10},{13,12},{15,14},{17,16},{19,... | collective-permute-start | bytes 1572872 | tf_op jit(solution)/shard_map/ppermute | solution.py:308
  37.4 22.4 %collective-permute-start.6 = (bf16[2,128,1024]{2,1,0:T(8,128)(2,1)}, bf16[2,128,1024]{2,1,0:T(8,128)(2,1)}, u32[]{:S(2)}, u32[]{:S(2)}) collective-permute-start(bf16[2,128,1024]{2,1,0:T(8,128)(2,1)} %get-tuple-element.5), channel_id=1, source_target_pairs={{4,1},{6,3},{8,5},{10,7},{12,9},{14,11},{20,17},{22,19},{24,21},{2... | collective-permute-start | bytes 1572872 | tf_op jit(solution)/shard_map/ppermute | solution.py:308
  38.7 0.8 copy-start.4
  39.5 20.3 %collective-permute-start.3 = (bf16[2,128,1024]{2,1,0:T(8,128)(2,1)}, bf16[2,128,1024]{2,1,0:T(8,128)(2,1)S(1)}, u32[]{:S(2)}, u32[]{:S(2)}) collective-permute-start(bf16[2,128,1024]{2,1,0:T(8,128)(2,1)} %shard_map.69.next_amp), channel_id=1, source_target_pairs={{0,1},{1,0},{2,3},{3,2},{4,5},{5,4},{6,7},{7,6},{8,9},{9,8},{10,11... | collective-permute-start | bytes 1572872 | tf_op jit(solution)/shard_map/ppermute | solution.py:308
  43.9 15.9 %collective-permute-start.5 = (bf16[2,128,1024]{2,1,0:T(8,128)(2,1)S(1)}, bf16[2,128,1024]{2,1,0:T(8,128)(2,1)}, u32[]{:S(2)}, u32[]{:S(2)}) collective-permute-start(bf16[2,128,1024]{2,1,0:T(8,128)(2,1)S(1)} %collective-permute-done.4.next_phase), channel_id=1, source_target_pairs={{0,1},{1,0},{2,3},{3,2},{4,5},{5,4},{6,7},{7,6},{8,9},{9,8},{10,11... | collective-permute-start | bytes 1572872 | tf_op jit(solution)/shard_map/ppermute | solution.py:308
  55.3 9.2 %collective-permute-start.7 = (f32[64,1024]{1,0:T(8,128)S(1)}, f32[64,1024]{1,0:T(8,128)S(1)}, u32[]{:S(2)}, u32[]{:S(2)}) collective-permute-start(f32[64,1024]{1,0:T(8,128)S(1)} %bitcast.5), channel_id=1, source_target_pairs={{0,1},{1,0},{2,3},{3,2},{4,5},{5,4},{6,7},{7,6},{8,9},{9,8},{10,11... | collective-permute-start | bytes 786440 | tf_op jit(solution)/shard_map/ppermute | solution.py:308
  57.1 1.0 %copy-start.5 = (bf16[2,128,1024]{2,1,0:T(8,128)(2,1)S(1)}, bf16[2,128,1024]{2,1,0:T(8,128)(2,1)}, u32[]{:S(2)}) copy-start(bf16[2,128,1024]{2,1,0:T(8,128)(2,1)} %shard_map.69.next_amp) | copy-start | bytes 1572868
  59.8 4.8 %copy-start.6 = (s32[2]{0:T(128)S(1)}, s32[2]{0:T(128)}, u32[]{:S(2)}) copy-start(s32[2]{0:T(128)} %pad_add_fusion.place_ref) | copy-start | bytes 28
  59.8 4.8 %copy-start.7 = (s32[128,1024]{1,0:T(8,128)S(1)}, s32[128,1024]{1,0:T(8,128)}, u32[]{:S(2)}) copy-start(s32[128,1024]{1,0:T(8,128)} %half_ref.1) | copy-start | bytes 1572868
  59.8 4.8 %copy-start.8 = (bf16[3,128,256]{2,1,0:T(8,128)(2,1)S(1)}, bf16[3,128,256]{2,1,0:T(8,128)(2,1)}, u32[]{:S(2)}) copy-start(bf16[3,128,256]{2,1,0:T(8,128)(2,1)} %constant.43.clone.band_ref) | copy-start | bytes 589828
